TPU v7x, 32 devices: a whole 2x2x4 slice. The times are simulated.
32 devices in a mesh: groups: 2 (over y), wide: 4 (over z), narrow: 4 (over x, core).
Axes of the slice: x: 2, y: 2, z: 4, core: 2. Of those that a mesh axis runs over, the one named last changes fastest.
Arguments:
- hidden: bfloat16 [32, 8192], P('groups', 'wide'), parts along dimension 0, may hold values from -6 to 6
- w_query: bfloat16 [8192, 8192], P('wide', 'narrow'), may hold values from -0.0625 to 0.0625
- w_key: bfloat16 [8192, 1024], P('wide', 'narrow'), may hold values from -0.0625 to 0.0625
- w_value: bfloat16 [8192, 1024], P('wide', 'narrow'), may hold values from -0.0625 to 0.0625
- w_out: bfloat16 [8192, 8192], P('narrow', 'wide'), may hold values from -0.0625 to 0.0625
- key_cache: bfloat16 [32, 768, 8, 128], P(('groups', 'wide'), None, 'narrow'), parts along dimension 0, may hold values from -720 to 720
- value_cache: bfloat16 [32, 768, 8, 128], P(('groups', 'wide'), None, 'narrow'), parts along dimension 0, may hold values from -6 to 6
- cycle_offset: int32 [32], P(('groups', 'wide')), parts along dimension 0, may hold values from 0 to 767
- valid_length: int32 [32], P(('groups', 'wide')), parts along dimension 0, may hold values from 1 to 768, as said below
- slot_of: int32 [32], P('groups'), parts along dimension 0, may hold values from 0 to 15, as said below
Outputs:
- attn_out: bfloat16 [32, 8192], P('groups', 'wide'), parts along dimension 0
- new_keys: bfloat16 [32, 1024], P(('groups', 'wide'), 'narrow'), parts along dimension 0
- new_values: bfloat16 [32, 1024], P(('groups', 'wide'), 'narrow'), parts along dimension 0
There are 2 independent parts, one for each index of `groups`. A program takes and returns all parts, laid end to end along the dimension named above; an argument that names none is the same for every part. Nothing has to cross between parts.
Inputs may be any that keep to these rules, and one draw needn't show every extreme that they name: Requests are in 4 microbatches of consecutive rows; each cache owner (a block of 4 consecutive slots) holds exactly 1 request of each microbatch m, at the slots owner * 4 + m + j for 0 <= j < 1; slot_of is a permutation. `valid_length`: at least one slot has a full cycle.
All inputs are finite; a program needn't handle non-finite values.
Results may differ from a plain program's by a relative error of at most 0.012.
Values may be sent and summed in bfloat16 or wider, within the bound.
No kernel may reach another device: no remote copies, remote signals or barrier semaphores. Data moves between devices by JAX's collectives and lax.ppermute only.
A program may use at most 64 MiB of HBM per device.

v0:
```python
import jax
import jax.numpy as jnp
from jax import lax
from jax.sharding import PartitionSpec as P

masked_low = -1e30


def attend(queries, keys_new, values_new, key_cache, value_cache, offset, length):
    slots, window, kv_local, head_dim = key_cache.shape
    group = queries.shape[1] // (kv_local * head_dim)
    scale = 1.0 / jnp.sqrt(jnp.float32(head_dim))
    query_heads = queries.reshape(slots, kv_local, group, head_dim)
    key_heads = keys_new.reshape(slots, kv_local, head_dim)
    value_heads = values_new.reshape(slots, kv_local, head_dim)
    cached = (
        jnp.einsum("skgd,sjkd->skgj", query_heads, key_cache, preferred_element_type=jnp.float32)
        * scale
    )
    fresh = (
        jnp.einsum("skgd,skd->skg", query_heads, key_heads, preferred_element_type=jnp.float32)
        * scale
    )
    distance = (offset[:, None] - jnp.arange(window, dtype=jnp.int32)[None, :]) % window
    usable = ((distance > 0) & (distance < length[:, None]))[:, None, None, :]
    masked = jnp.where(usable, cached, masked_low)
    top = jnp.maximum(jnp.max(masked, axis=3), fresh)
    spread = jnp.where(usable, jnp.exp(masked - top[..., None]), 0.0)
    own = jnp.exp(fresh - top)
    total = jnp.sum(spread, axis=3) + own
    weights = (spread / total[..., None]).astype(jnp.bfloat16)
    own_weight = (own / total).astype(jnp.bfloat16)
    mixed = jnp.einsum("skgj,sjkd->skgd", weights, value_cache, preferred_element_type=jnp.float32)
    mixed = (
        mixed
        + own_weight.astype(jnp.float32)[..., None] * value_heads.astype(jnp.float32)[:, :, None, :]
    )
    return mixed.astype(jnp.bfloat16).reshape(slots, -1)


def per_device(
    hidden,
    w_query,
    w_key,
    w_value,
    w_out,
    key_cache,
    value_cache,
    cycle_offset,
    valid_length,
    slot_of,
):
    requests = slot_of.shape[0]
    slots_dev = key_cache.shape[0]
    query_cols = w_query.shape[1]
    key_cols = w_key.shape[1]
    order = jnp.zeros((requests,), jnp.int32).at[slot_of].set(jnp.arange(requests, dtype=jnp.int32))
    rows = hidden[order[jnp.arange(slots_dev * lax.axis_size("wide"), dtype=jnp.int32)]]
    summed = lax.psum_scatter(
        jnp.concatenate(
            [
                jnp.dot(rows, w_query, preferred_element_type=jnp.float32),
                jnp.dot(rows, w_key, preferred_element_type=jnp.float32),
                jnp.dot(rows, w_value, preferred_element_type=jnp.float32),
            ],
            axis=1,
        ),
        "wide",
        scatter_dimension=0,
        tiled=True,
    )
    fresh = summed.astype(jnp.bfloat16)
    queries = fresh[:, :query_cols]
    keys_out = fresh[:, query_cols : query_cols + key_cols]
    values_out = fresh[:, query_cols + key_cols :]
    heads = attend(
        queries, keys_out, values_out, key_cache, value_cache, cycle_offset, valid_length
    )
    slot_out = jnp.dot(
        lax.all_gather(heads, "wide", axis=0, tiled=True), w_out, preferred_element_type=jnp.float32
    )
    request_out = slot_out[slot_of]
    attn_out = lax.psum(request_out, "narrow").astype(jnp.bfloat16)
    return (attn_out, keys_out, values_out)


def solution(mesh):
    placed = (
        P("groups", "wide"),
        P("wide", "narrow"),
        P("wide", "narrow"),
        P("wide", "narrow"),
        P("narrow", "wide"),
        P(("groups", "wide"), None, "narrow", None),
        P(("groups", "wide"), None, "narrow", None),
        P(("groups", "wide")),
        P(("groups", "wide")),
        P("groups"),
    )
    return jax.shard_map(
        per_device,
        mesh=mesh,
        in_specs=placed,
        out_specs=(
            P("groups", "wide"),
            P(("groups", "wide"), "narrow"),
            P(("groups", "wide"), "narrow"),
        ),
        check_vma=False,
    )
```

profile of v0, /device:TPU:0, one launch (start us, length us, event | category | flops | bytes accessed | tf_op | source)
XLA Modules:
  0.0 66.6 jit_solution(1026639459956276129)
XLA Ops:
  0.6 0.0 copy-start
  0.6 0.8 %compare_select_fusion.1 = s32[16]{0:T(128)S(1)} fusion(s32[16]{0:T(128)} %param.19), kind=kLoop, calls=%fused_computation.40 | loop fusion | flops 48 | bytes 128 | tf_op jit(solution)/shard_map/select_n | solution.py:57
  1.4 0.6 scatter_custom_fusion
  2.1 0.7 gather_fusion
  2.8 1.5 %gather_fusion.1 = bf16[16,2048]{1,0:T(8,128)(2,1)S(1)} fusion(bf16[16,2048]{1,0:T(8,128)(2,1)} %param.10, s32[1024]{0:T(1024)S(1)} %pad_clamp_fusion.1), kind=kCustom, calls=%fused_computation.1 | custom fusion | bytes 131136 | tf_op jit(solution)/shard_map/gather | solution.py:58
  4.3 0.0 copy-start.1
  4.3 0.0 copy-start.2
  4.3 4.7 %fusion.37 = f32[16,2048]{1,0:T(8,128)S(1)} fusion(bf16[16,2048]{1,0:T(8,128)(2,1)S(1)} %gather_fusion.1, bf16[2048,2048]{1,0:T(8,128)(2,1)} %param.11), kind=kOutput, calls=%fused_computation.49 | convolution fusion | flops 134217728 | bytes 8585216 | tf_op jit(solution)/shard_map/dot_general | solution.py:62
  9.0 0.0 copy-done.1
  9.0 0.0 copy-start.5
  9.0 0.0 copy-start.6
  9.0 0.2 fusion.38
  9.3 0.0 copy-done.2
  9.3 0.3 fusion.39
  9.6 23.7 %all-reduce.3 = bf16[16,2560]{1,0:T(8,128)(2,1)S(1)} all-reduce(f32[16,2560]{1,0:T(8,128)S(1)} %pad_maximum_fusion), channel_id=2, replica_groups=mesh['groups'=2,'wide'=4,'narrow'=4] {'wide'}, use_global_device_ids=true, to_apply=%region_1.0.clone | all-reduce | flops 40960 | bytes 245760
  33.3 0.0 copy-done.8
  33.3 0.6 dynamic-slice
  34.6 0.0 copy-start.3
  34.6 0.0 copy-start.4
  34.7 0.1 fusion.21
  34.8 0.0 copy-done.5
  34.8 0.0 copy-done.6
  34.8 0.1 compare_and_fusion
  34.9 0.0 copy-done
  34.9 0.6 fusion.36
  35.5 0.2 fusion.16
  35.8 0.4 fusion.13
  36.2 0.0 copy-done.4
  36.2 13.2 %all-gather = bf16[4,4,2048]{2,1,0:T(4,128)(2,1)S(1)} all-gather(bf16[1,4,2048]{2,1,0:T(4,128)(2,1)S(1)} %reshape.114), channel_id=1, replica_groups=mesh['groups'=2,'wide'=4,'narrow'=4] {'wide'}, dimensions={0}, use_global_device_ids=true | all-gather | bytes 81920 | tf_op jit(solution)/shard_map/all_gather | solution.py:80
  49.4 4.6 %fusion.40 = f32[16,2048]{1,0:T(8,128)S(1)} fusion(bf16[16,2048]{1,0:T(8,128)(2,1)S(1)} %reshape.115, bf16[2048,2048]{1,0:T(8,128)(2,1)} %param.14), kind=kOutput, calls=%fused_computation.52 | convolution fusion | flops 134217728 | bytes 8585216 | tf_op jit(solution)/shard_map/dot_general | solution.py:79
  53.9 0.6 gather_fusion.2
  54.6 12.0 %all-reduce.4 = bf16[16,2048]{1,0:T(8,128)(2,1)} all-reduce(f32[16,2048]{1,0:T(8,128)S(1)} %gather_fusion.2), channel_id=1, replica_groups=mesh['groups'=2,'wide'=4,'narrow'=4] {'narrow'}, use_global_device_ids=true, to_apply=%region_4.5 | all-reduce | flops 32768 | bytes 196608 | tf_op jit(solution)/shard_map/psum | solution.py:83
  (20 shorter events, 0.2 us)
Async XLA Ops:
  0.6 34.3 %copy-start = (bf16[4,768,2,128]{3,2,1,0:T(2,128)(2,1)S(1)}, bf16[4,768,2,128]{3,2,1,0:T(2,128)(2,1)}, u32[]{:S(2)}) copy-start(bf16[4,768,2,128]{3,2,1,0:T(2,128)(2,1)} %param.15) | copy-start | bytes 4718596
  4.3 4.7 %copy-start.1 = (bf16[2048,256]{1,0:T(8,128)(2,1)S(1)}, bf16[2048,256]{1,0:T(8,128)(2,1)}, u32[]{:S(2)}) copy-start(bf16[2048,256]{1,0:T(8,128)(2,1)} %param.12) | copy-start | bytes 3145732
  4.3 5.0 %copy-start.2 = (bf16[2048,256]{1,0:T(8,128)(2,1)S(1)}, bf16[2048,256]{1,0:T(8,128)(2,1)}, u32[]{:S(2)}) copy-start(bf16[2048,256]{1,0:T(8,128)(2,1)} %param.13) | copy-start | bytes 3145732
  9.0 24.3 %copy-start.8 = (u32[32]{0:T(128)S(1)}, u32[32]{0:T(128)}, u32[]{:S(2)}) copy-start(u32[32]{0:T(128)} %constant.32) | copy-start | bytes 388
  9.0 25.8 %copy-start.5 = (s32[4]{0:T(128)S(1)}, s32[4]{0:T(128)}, u32[]{:S(2)}) copy-start(s32[4]{0:T(128)} %param.18) | copy-start | bytes 52
  9.0 25.8 %copy-start.6 = (s32[4]{0:T(128)S(1)}, s32[4]{0:T(128)}, u32[]{:S(2)}) copy-start(s32[4]{0:T(128)} %param.17) | copy-start | bytes 52
  9.6 26.2 %copy-start.7 = (bf16[4,768,2,128]{3,2,1,0:T(2,128)(2,1)S(1)}, bf16[4,768,2,128]{3,2,1,0:T(2,128)(2,1)}, u32[]{:S(2)}) copy-start(bf16[4,768,2,128]{3,2,1,0:T(2,128)(2,1)} %param.16) | copy-start | bytes 4718596
  34.6 1.6 %copy-start.3 = (bf16[4,256]{1,0:T(4,128)(2,1)}, bf16[4,256]{1,0:T(4,128)(2,1)S(1)}, u32[]{:S(2)}) copy-start(bf16[4,256]{1,0:T(4,128)(2,1)S(1)} %get-tuple-element.3) | copy-start | bytes 6148
  34.6 1.5 %copy-start.4 = (bf16[4,256]{1,0:T(4,128)(2,1)}, bf16[4,256]{1,0:T(4,128)(2,1)S(1)}, u32[]{:S(2)}) copy-start(bf16[4,256]{1,0:T(4,128)(2,1)S(1)} %get-tuple-element.4) | copy-start | bytes 6148
where the time goes:
time: 66.8 us; the launch traced here: 66.6 us
  blocking collectives  48.9 us (73%)
  matrix products  10.9 us (16%)
  local copies, waits for them, and re-layouts  4.13 us (6%)
  between operations  1.5 us (2%)
  other arithmetic  1.13 us (2%)
    unnamed x1, blocking collectives  23.7 us
    all_gather x1, blocking collectives, per_device(): lax.all_gather(heads, 'wide', axis=0, tiled=True)  13.2 us
    psum x1, blocking collectives, per_device(): attn_out = lax.psum(request_out, 'narrow').astype(jnp.bfloat16)  12 us
    dot_general x1, matrix products, per_device(): jnp.dot(rows, w_query, preferred_element_type=jnp.float32)  4.72 us
    dot_general x1, matrix products, per_device(): jnp.dot(lax.all_gather(heads, 'wide', axis=0, tiled=True), w_out, preferr...  4.58 us
    gather x1, local copies, waits for them, and re-layouts, per_device(): hidden[order[jnp.arange(slots_dev * lax.axis_size('wide'), dtype=jnp.int3...  1.51 us

commit v1 on v0

--- a/solution.py
+++ b/solution.py
@@ -4,6 +4,22 @@
 from jax.sharding import PartitionSpec as P
 
 masked_low = -1e30
+most_direct = 8
+
+
+def is_direct(count):
+    return count <= most_direct and count & (count - 1) == 0
+
+
+def swap(block, axis, distance):
+    count = lax.axis_size(axis)
+    return lax.ppermute(block, axis, [(i, i ^ distance) for i in range(count)])
+
+
+def tree_sum(terms):
+    while len(terms) > 1:
+        terms = [a + b for a, b in zip(terms[::2], terms[1::2])]
+    return terms[0]
 
 
 def attend(queries, keys_new, values_new, key_cache, value_cache, offset, length):
@@ -54,21 +70,34 @@
     slots_dev = key_cache.shape[0]
     query_cols = w_query.shape[1]
     key_cols = w_key.shape[1]
-    order = jnp.zeros((requests,), jnp.int32).at[slot_of].set(jnp.arange(requests, dtype=jnp.int32))
-    rows = hidden[order[jnp.arange(slots_dev * lax.axis_size("wide"), dtype=jnp.int32)]]
-    summed = lax.psum_scatter(
-        jnp.concatenate(
-            [
-                jnp.dot(rows, w_query, preferred_element_type=jnp.float32),
-                jnp.dot(rows, w_key, preferred_element_type=jnp.float32),
-                jnp.dot(rows, w_value, preferred_element_type=jnp.float32),
-            ],
-            axis=1,
-        ),
-        "wide",
-        scatter_dimension=0,
-        tiled=True,
+    wide = lax.axis_size("wide")
+    direct_wide = is_direct(wide)
+    place = jnp.arange(requests, dtype=jnp.int32)
+    if direct_wide:
+        me = lax.axis_index("wide")
+        slot_at = (me ^ (place // slots_dev)) * slots_dev + place % slots_dev
+    else:
+        slot_at = place
+    picks = (slot_at[:, None] == slot_of[None, :]).astype(jnp.bfloat16)
+    rows = jnp.dot(picks, hidden, preferred_element_type=jnp.float32).astype(jnp.bfloat16)
+    parts = jnp.concatenate(
+        [
+            jnp.dot(rows, w_query, preferred_element_type=jnp.float32),
+            jnp.dot(rows, w_key, preferred_element_type=jnp.float32),
+            jnp.dot(rows, w_value, preferred_element_type=jnp.float32),
+        ],
+        axis=1,
     )
+    if direct_wide:
+        summed = tree_sum(
+            [parts[:slots_dev]]
+            + [
+                swap(parts[d * slots_dev : (d + 1) * slots_dev], "wide", d)
+                for d in range(1, wide)
+            ]
+        )
+    else:
+        summed = lax.psum_scatter(parts, "wide", scatter_dimension=0, tiled=True)
     fresh = summed.astype(jnp.bfloat16)
     queries = fresh[:, :query_cols]
     keys_out = fresh[:, query_cols : query_cols + key_cols]
@@ -76,12 +105,22 @@
     heads = attend(
         queries, keys_out, values_out, key_cache, value_cache, cycle_offset, valid_length
     )
-    slot_out = jnp.dot(
-        lax.all_gather(heads, "wide", axis=0, tiled=True), w_out, preferred_element_type=jnp.float32
-    )
-    request_out = slot_out[slot_of]
-    attn_out = lax.psum(request_out, "narrow").astype(jnp.bfloat16)
-    return (attn_out, keys_out, values_out)
+    if direct_wide:
+        heads = jnp.concatenate([heads] + [swap(heads, "wide", d) for d in range(1, wide)], axis=0)
+    else:
+        heads = lax.all_gather(heads, "wide", axis=0, tiled=True)
+    heads = jnp.dot(picks.T, heads, preferred_element_type=jnp.float32).astype(jnp.bfloat16)
+    request_out = jnp.dot(heads, w_out, preferred_element_type=jnp.float32)
+    narrow = lax.axis_size("narrow")
+    if is_direct(narrow):
+        sent = request_out.astype(jnp.bfloat16)
+        attn_out = tree_sum(
+            [sent.astype(jnp.float32)]
+            + [swap(sent, "narrow", d).astype(jnp.float32) for d in range(1, narrow)]
+        )
+    else:
+        attn_out = lax.psum(request_out, "narrow")
+    return (attn_out.astype(jnp.bfloat16), keys_out, values_out)
 
 
 def solution(mesh):

time: 66.8 us -> 38.2 us (0.57)
  blocking collectives: 48.9 us -> 0 us
  starting transfers between devices: 0 us -> 12 us
  waiting for transfers between devices: 0 us -> 11.7 us
  local copies, waits for them, and re-layouts: 4.13 us -> 0.12 us
  matrix products: 10.9 us -> 12.3 us
  between operations: 1.5 us -> 0.8 us
    unnamed x1 -> x0, blocking collectives: 23.7 us -> none
    all_gather x1 -> x0, blocking collectives: 13.2 us -> none  [per_device(): lax.all_gather(heads, 'wide', axis=0, tiled=True)]
    psum x1 -> x0, blocking collectives: 12 us -> none  [per_device(): attn_out = lax.psum(request_out, 'narrow').astype(jnp.bfloat16)]
    ppermute x0 -> x9, starting transfers between devices: none -> 12 us  [swap(): return lax.ppermute(block, axis, [(i, i ^ distance) for i in range(count)])]
    ppermute x0 -> x9, waiting for transfers between devices: none -> 11.7 us  [swap(): return lax.ppermute(block, axis, [(i, i ^ distance) for i in range(count)])]
    gather x3 -> x0, local copies, waits for them, and re-layouts: 2.77 us -> none  [the longest x1 1.51 us: per_device(): hidden[order[jnp.arange(slots_dev * lax.axis_size('wide'), dtype=jnp.int3...]
    dot_general x1 -> x2, matrix products: 4.58 us -> 5.98 us  [the longest x1 4.81 us: per_device(): request_out = jnp.dot(heads, w_out, preferred_element_type=jnp.float32)]
    select_n x2 -> x0, other arithmetic: 0.78 us -> none  [the longest x1 0.78 us: per_device(): jnp.zeros((requests,), jnp.int32).at[slot_of]]
  transfers between devices with their start and end apart: 0 -> 9, of which waited for: 0 -> 6; matrix products, arithmetic and copies ran while one was open for 0% -> 0% of each run, Pallas kernels for 0% -> 0%
where the time goes in v1:
time: 38.2 us; the launch traced here: 38 us
  matrix products  12.3 us (32%)
  starting transfers between devices  12 us (31%)
  waiting for transfers between devices  11.7 us (31%)
  other arithmetic  1.02 us (3%)
  between operations  0.8 us (2%)
    ppermute x9, starting transfers between devices, swap(): return lax.ppermute(block, axis, [(i, i ^ distance) for i in range(count)])  12 us
    ppermute x9, waiting for transfers between devices, swap(): return lax.ppermute(block, axis, [(i, i ^ distance) for i in range(count)])  11.7 us
    dot_general x1, matrix products, per_device(): request_out = jnp.dot(heads, w_out, preferred_element_type=jnp.float32)  4.81 us
    dot_general x1, matrix products, per_device(): jnp.dot(rows, w_query, preferred_element_type=jnp.float32)  4.73 us
    dot_general x1, matrix products, per_device(): jnp.dot(picks, hidden, preferred_element_type=jnp.float32)  1.17 us
  transfers between devices with their start and end apart: 9, of which 6 were waited for; matrix products, arithmetic and copies ran while one was open for 0% of the time, Pallas kernels for 0%

profile of v1, /device:TPU:0, one launch (start us, length us, event | category | flops | bytes accessed | tf_op | source)
XLA Modules:
  0.0 38.0 jit_solution(18062829371433969959)
XLA Ops:
  0.6 0.0 copy-start
  0.7 1.2 %convolution_convert_fusion.1 = bf16[16,2048]{1,0:T(8,128)(2,1)S(1)} fusion(bf16[16,2048]{1,0:T(8,128)(2,1)} %param.10, s32[16]{0:T(128)} %param.19, s32[16]{0:T(128)S(1)} %fusion.58), kind=kOutput, calls=%fused_computation.1 | convolution fusion | flops 1081600 | bytes 131200 | tf_op jit(solution)/shard_map/dot_general | solution.py:82
  1.8 0.0 copy-start.1
  1.8 0.0 copy-start.2
  1.9 4.7 %fusion.68 = f32[16,2048]{1,0:T(8,128)S(1)} fusion(bf16[16,2048]{1,0:T(8,128)(2,1)S(1)} %convolution_convert_fusion.1, bf16[2048,2048]{1,0:T(8,128)(2,1)} %param.11), kind=kOutput, calls=%fused_computation.68 | convolution fusion | flops 134217728 | bytes 8585216 | tf_op jit(solution)/shard_map/dot_general | solution.py:85
  6.6 0.0 copy-start.7
  6.6 0.2 fusion.69
  6.9 0.3 fusion.70
  7.2 3.1 %collective-permute-start = (f32[4,2560]{1,0:T(4,128)S(1)}, f32[4,2560]{1,0:T(4,128)S(1)}, u32[]{:S(2)}, u32[]{:S(2)}) collective-permute-start(f32[4,2560]{1,0:T(4,128)S(1)} %get-tuple-element.5), channel_id=1, source_target_pairs={{0,4},{4,0},{8,12},{12,8},{1,5},{5,1},{9,13},{13,9},{2,6},{6,2},{1... | collective-permute-start | bytes 122888 | tf_op jit(solution)/shard_map/ppermute | solution.py:16
  10.3 2.6 %collective-permute-start.1 = (f32[4,2560]{1,0:T(4,128)S(1)}, f32[4,2560]{1,0:T(4,128)S(1)}, u32[]{:S(2)}, u32[]{:S(2)}) collective-permute-start(f32[4,2560]{1,0:T(4,128)S(1)} %get-tuple-element.4), channel_id=1, source_target_pairs={{0,8},{4,12},{8,0},{12,4},{1,9},{5,13},{9,1},{13,5},{2,10},{6,14},... | collective-permute-start | bytes 122888 | tf_op jit(solution)/shard_map/ppermute | solution.py:16
  12.9 0.1 compare_and_fusion
  12.9 0.0 collective-permute-done
  13.0 3.0 %collective-permute-done.1 = f32[4,2560]{1,0:T(4,128)S(1)} collective-permute-done((f32[4,2560]{1,0:T(4,128)S(1)}, f32[4,2560]{1,0:T(4,128)S(1)}, u32[]{:S(2)}, u32[]{:S(2)}) %collective-permute-start.1) | collective-permute-done | bytes 40992 | tf_op jit(solution)/shard_map/ppermute | solution.py:16
  15.9 2.7 %collective-permute-done.2 = f32[4,2560]{1,0:T(4,128)S(1)} collective-permute-done((f32[4,2560]{1,0:T(4,128)S(1)}, f32[4,2560]{1,0:T(4,128)S(1)}, u32[]{:S(2)}, u32[]{:S(2)}) %collective-permute-start.2) | collective-permute-done | bytes 40992 | tf_op jit(solution)/shard_map/ppermute | solution.py:16
  18.7 0.0 copy-start.3
  18.7 0.0 copy-start.4
  18.7 0.1 fusion.40
  18.9 0.6 %fusion.67 = (f32[4,2,8]{2,1,0:T(2,128)S(1)}, f32[4,2,8,768]{3,2,1,0:T(8,128)S(1)}) fusion(bf16[4,768,2,128]{3,2,1,0:T(2,128)(2,1)S(1)} %copy-done, bf16[1,4,16,128]{3,1,2,0:T(4,128)(2,1)S(1)} %slice_bitcast_fusion, pred[4,768]{1,0:T(4,128)(4,1)S(1)} %compare_and_fusion), kind=kOutput, calls=%fused_computation.67 | convolution fusion | flops 12730304 | bytes 1789184 | tf_op jit(solution)/shard_map/skgd,sjkd->skgj/dot_general | solution.py:33
  19.5 0.2 fusion.19
  19.7 0.4 %fusion.16 = bf16[1,4,16,128]{3,2,1,0:T(8,128)(2,1)S(1)} fusion(bf16[4,768,2,128]{3,2,1,0:T(2,128)(2,1)S(1)} %copy-done.8, f32[4,2,8,768]{3,2,1,0:T(8,128)S(1)} %get-tuple-element.11, f32[4,2,8]{2,1,0:T(2,128)S(1)} %get-tuple-element.9, f32[4,2,8]{2,1,0:T(2,128)S(1)} %multiply_maximum_fusion, pred[4,768]{1,0:T(4,128)(4,1)S(1)} %compare_and_fusion, ...), kind=kOutput, calls=%fused_computation.11 | convolution fusion | flops 12804096 | bytes 1793792 | tf_op jit(solution)/shard_map/skgj,sjkd->skgd/dot_general | solution.py:49
  20.1 0.0 copy-done.4
  20.1 0.1 collective-permute-start.3
  20.2 1.1 %collective-permute-start.4 = (bf16[4,2048]{1,0:T(4,128)(2,1)S(1)}, bf16[4,2048]{1,0:T(4,128)(2,1)S(1)}, u32[]{:S(2)}, u32[]{:S(2)}) collective-permute-start(bf16[4,2048]{1,0:T(4,128)(2,1)S(1)} %bitcast.28), channel_id=1, source_target_pairs={{0,8},{4,12},{8,0},{12,4},{1,9},{5,13},{9,1},{13,5},{2,10},{6,14},... | collective-permute-start | bytes 49160 | tf_op jit(solution)/shard_map/ppermute | solution.py:16
  21.3 3.3 %collective-permute-start.5 = (bf16[4,2048]{1,0:T(4,128)(2,1)S(1)}, bf16[4,2048]{1,0:T(4,128)(2,1)S(1)}, u32[]{:S(2)}, u32[]{:S(2)}) collective-permute-start(bf16[4,2048]{1,0:T(4,128)(2,1)S(1)} %bitcast.29), channel_id=1, source_target_pairs={{0,12},{4,8},{8,4},{12,0},{1,13},{5,9},{9,5},{13,1},{2,14},{6,10},... | collective-permute-start | bytes 49160 | tf_op jit(solution)/shard_map/ppermute | solution.py:16
  24.6 0.3 collective-permute-done.4
  24.9 1.9 %collective-permute-done.5 = bf16[4,2048]{1,0:T(4,128)(2,1)S(1)} collective-permute-done((bf16[4,2048]{1,0:T(4,128)(2,1)S(1)}, bf16[4,2048]{1,0:T(4,128)(2,1)S(1)}, u32[]{:S(2)}, u32[]{:S(2)}) %collective-permute-start.5) | collective-permute-done | bytes 16416 | tf_op jit(solution)/shard_map/ppermute | solution.py:16
  26.9 4.8 %convolution_convert_fusion.2 = bf16[16,2048]{1,0:T(8,128)(2,1)S(1)} fusion(bf16[2048,2048]{1,0:T(8,128)(2,1)} %param.14, bf16[4,2048]{1,0:T(4,128)(2,1)S(1)} %collective-permute-done.5, bf16[4,2048]{1,0:T(4,128)(2,1)S(1)} %collective-permute-done.4, bf16[4,2048]{1,0:T(4,128)(2,1)S(1)} %collective-permute-done.3, bf16[4,2048]{1,0:T(4,128)(2,1)S(1)} %bitcast.30, ...), kind=kOutput, calls=%fused_computation.2 | convolution fusion | flops 135594240 | bytes 8519808 | tf_op jit(solution)/shard_map/dot_general | solution.py:113
  31.7 1.5 %collective-permute-start.7 = (bf16[16,2048]{1,0:T(8,128)(2,1)S(1)}, bf16[16,2048]{1,0:T(8,128)(2,1)S(1)}, u32[]{:S(2)}, u32[]{:S(2)}) collective-permute-start(bf16[16,2048]{1,0:T(8,128)(2,1)S(1)} %convolution_convert_fusion.2), channel_id=1, source_target_pairs={{0,2},{1,3},{2,0},{3,1},{4,6},{5,7},{6,4},{7,5},{8,10},{9,11},{10,... | collective-permute-start | bytes 196616 | tf_op jit(solution)/shard_map/ppermute | solution.py:16
  33.2 0.3 collective-permute-start.8
  33.5 2.6 %collective-permute-done.7 = bf16[16,2048]{1,0:T(8,128)(2,1)S(1)} collective-permute-done((bf16[16,2048]{1,0:T(8,128)(2,1)S(1)}, bf16[16,2048]{1,0:T(8,128)(2,1)S(1)}, u32[]{:S(2)}, u32[]{:S(2)}) %collective-permute-start.7) | collective-permute-done | bytes 65568 | tf_op jit(solution)/shard_map/ppermute | solution.py:16
  36.2 1.1 %collective-permute-done.8 = bf16[16,2048]{1,0:T(8,128)(2,1)S(1)} collective-permute-done((bf16[16,2048]{1,0:T(8,128)(2,1)S(1)}, bf16[16,2048]{1,0:T(8,128)(2,1)S(1)}, u32[]{:S(2)}, u32[]{:S(2)}) %collective-permute-start.8) | collective-permute-done | bytes 65568 | tf_op jit(solution)/shard_map/ppermute | solution.py:16
  37.3 0.7 %add_convert_fusion = bf16[16,2048]{1,0:T(8,128)(2,1)} fusion(bf16[16,2048]{1,0:T(8,128)(2,1)S(1)} %collective-permute-done.8, bf16[16,2048]{1,0:T(8,128)(2,1)S(1)} %collective-permute-done.7, bf16[16,2048]{1,0:T(8,128)(2,1)S(1)} %collective-permute-done.6, bf16[16,2048]{1,0:T(8,128)(2,1)S(1)} %convolution_convert_fusion.2), kind=kLoop, calls=%fused_computation.16 | loop fusion | flops 262144 | bytes 327680 | tf_op jit(solution)/shard_map/convert_element_type | solution.py:123
  (26 shorter events, 0.2 us)
Async XLA Ops:
  0.6 18.2 %copy-start = (bf16[4,768,2,128]{3,2,1,0:T(2,128)(2,1)S(1)}, bf16[4,768,2,128]{3,2,1,0:T(2,128)(2,1)}, u32[]{:S(2)}) copy-start(bf16[4,768,2,128]{3,2,1,0:T(2,128)(2,1)} %param.15) | copy-start | bytes 4718596
  1.8 4.8 %copy-start.1 = (bf16[2048,256]{1,0:T(8,128)(2,1)S(1)}, bf16[2048,256]{1,0:T(8,128)(2,1)}, u32[]{:S(2)}) copy-start(bf16[2048,256]{1,0:T(8,128)(2,1)} %param.12) | copy-start | bytes 3145732
  1.8 5.0 %copy-start.2 = (bf16[2048,256]{1,0:T(8,128)(2,1)S(1)}, bf16[2048,256]{1,0:T(8,128)(2,1)}, u32[]{:S(2)}) copy-start(bf16[2048,256]{1,0:T(8,128)(2,1)} %param.13) | copy-start | bytes 3145732
  6.6 6.3 %copy-start.6 = (s32[4]{0:T(128)S(1)}, s32[4]{0:T(128)}, u32[]{:S(2)}) copy-start(s32[4]{0:T(128)} %param.18) | copy-start | bytes 52
  6.6 6.3 %copy-start.7 = (s32[4]{0:T(128)S(1)}, s32[4]{0:T(128)}, u32[]{:S(2)}) copy-start(s32[4]{0:T(128)} %param.17) | copy-start | bytes 52
  7.1 12.6 %copy-start.8 = (bf16[4,768,2,128]{3,2,1,0:T(2,128)(2,1)S(1)}, bf16[4,768,2,128]{3,2,1,0:T(2,128)(2,1)}, u32[]{:S(2)}) copy-start(bf16[4,768,2,128]{3,2,1,0:T(2,128)(2,1)} %param.16) | copy-start | bytes 4718596
  7.2 5.8 %collective-permute-start = (f32[4,2560]{1,0:T(4,128)S(1)}, f32[4,2560]{1,0:T(4,128)S(1)}, u32[]{:S(2)}, u32[]{:S(2)}) collective-permute-start(f32[4,2560]{1,0:T(4,128)S(1)} %get-tuple-element.5), channel_id=1, source_target_pairs={{0,4},{4,0},{8,12},{12,8},{1,5},{5,1},{9,13},{13,9},{2,6},{6,2},{1... | collective-permute-start | bytes 122888 | tf_op jit(solution)/shard_map/ppermute | solution.py:16
  10.3 5.7 %collective-permute-start.1 = (f32[4,2560]{1,0:T(4,128)S(1)}, f32[4,2560]{1,0:T(4,128)S(1)}, u32[]{:S(2)}, u32[]{:S(2)}) collective-permute-start(f32[4,2560]{1,0:T(4,128)S(1)} %get-tuple-element.4), channel_id=1, source_target_pairs={{0,8},{4,12},{8,0},{12,4},{1,9},{5,13},{9,1},{13,5},{2,10},{6,14},... | collective-permute-start | bytes 122888 | tf_op jit(solution)/shard_map/ppermute | solution.py:16
  12.8 5.8 %collective-permute-start.2 = (f32[4,2560]{1,0:T(4,128)S(1)}, f32[4,2560]{1,0:T(4,128)S(1)}, u32[]{:S(2)}, u32[]{:S(2)}) collective-permute-start(f32[4,2560]{1,0:T(4,128)S(1)} %get-tuple-element.3), channel_id=1, source_target_pairs={{0,12},{4,8},{8,4},{12,0},{1,13},{5,9},{9,5},{13,1},{2,14},{6,10},... | collective-permute-start | bytes 122888 | tf_op jit(solution)/shard_map/ppermute | solution.py:16
  18.7 1.4 %copy-start.3 = (bf16[4,256]{1,0:T(4,128)(2,1)}, bf16[4,256]{1,0:T(4,128)(2,1)S(1)}, u32[]{:S(2)}) copy-start(bf16[4,256]{1,0:T(4,128)(2,1)S(1)} %get-tuple-element.6) | copy-start | bytes 6148
  18.7 1.4 %copy-start.4 = (bf16[4,256]{1,0:T(4,128)(2,1)}, bf16[4,256]{1,0:T(4,128)(2,1)S(1)}, u32[]{:S(2)}) copy-start(bf16[4,256]{1,0:T(4,128)(2,1)S(1)} %get-tuple-element.7) | copy-start | bytes 6148
  19.5 7.4 %copy-start.5 = (s32[16]{0:T(128)S(1)}, s32[16]{0:T(128)}, u32[]{:S(2)}) copy-start(s32[16]{0:T(128)} %param.19) | copy-start | bytes 196
  20.1 4.5 %collective-permute-start.3 = (bf16[4,2048]{1,0:T(4,128)(2,1)S(1)}, bf16[4,2048]{1,0:T(4,128)(2,1)S(1)}, u32[]{:S(2)}, u32[]{:S(2)}) collective-permute-start(bf16[4,2048]{1,0:T(4,128)(2,1)S(1)} %bitcast.27), channel_id=1, source_target_pairs={{0,4},{4,0},{8,12},{12,8},{1,5},{5,1},{9,13},{13,9},{2,6},{6,2},{1... | collective-permute-start | bytes 49160 | tf_op jit(solution)/shard_map/ppermute | solution.py:16
  20.2 4.7 %collective-permute-start.4 = (bf16[4,2048]{1,0:T(4,128)(2,1)S(1)}, bf16[4,2048]{1,0:T(4,128)(2,1)S(1)}, u32[]{:S(2)}, u32[]{:S(2)}) collective-permute-start(bf16[4,2048]{1,0:T(4,128)(2,1)S(1)} %bitcast.28), channel_id=1, source_target_pairs={{0,8},{4,12},{8,0},{12,4},{1,9},{5,13},{9,1},{13,5},{2,10},{6,14},... | collective-permute-start | bytes 49160 | tf_op jit(solution)/shard_map/ppermute | solution.py:16
  21.3 5.5 %collective-permute-start.5 = (bf16[4,2048]{1,0:T(4,128)(2,1)S(1)}, bf16[4,2048]{1,0:T(4,128)(2,1)S(1)}, u32[]{:S(2)}, u32[]{:S(2)}) collective-permute-start(bf16[4,2048]{1,0:T(4,128)(2,1)S(1)} %bitcast.29), channel_id=1, source_target_pairs={{0,12},{4,8},{8,4},{12,0},{1,13},{5,9},{9,5},{13,1},{2,14},{6,10},... | collective-permute-start | bytes 49160 | tf_op jit(solution)/shard_map/ppermute | solution.py:16
  31.7 1.9 %collective-permute-start.6 = (bf16[16,2048]{1,0:T(8,128)(2,1)S(1)}, bf16[16,2048]{1,0:T(8,128)(2,1)S(1)}, u32[]{:S(2)}, u32[]{:S(2)}) collective-permute-start(bf16[16,2048]{1,0:T(8,128)(2,1)S(1)} %convolution_convert_fusion.2), channel_id=1, source_target_pairs={{0,1},{1,0},{2,3},{3,2},{4,5},{5,4},{6,7},{7,6},{8,9},{9,8},{10,11... | collective-permute-start | bytes 196616 | tf_op jit(solution)/shard_map/ppermute | solution.py:16
  31.7 4.5 %collective-permute-start.7 = (bf16[16,2048]{1,0:T(8,128)(2,1)S(1)}, bf16[16,2048]{1,0:T(8,128)(2,1)S(1)}, u32[]{:S(2)}, u32[]{:S(2)}) collective-permute-start(bf16[16,2048]{1,0:T(8,128)(2,1)S(1)} %convolution_convert_fusion.2), channel_id=1, source_target_pairs={{0,2},{1,3},{2,0},{3,1},{4,6},{5,7},{6,4},{7,5},{8,10},{9,11},{10,... | collective-permute-start | bytes 196616 | tf_op jit(solution)/shard_map/ppermute | solution.py:16
  33.2 4.1 %collective-permute-start.8 = (bf16[16,2048]{1,0:T(8,128)(2,1)S(1)}, bf16[16,2048]{1,0:T(8,128)(2,1)S(1)}, u32[]{:S(2)}, u32[]{:S(2)}) collective-permute-start(bf16[16,2048]{1,0:T(8,128)(2,1)S(1)} %convolution_convert_fusion.2), channel_id=1, source_target_pairs={{0,3},{1,2},{2,1},{3,0},{4,7},{5,6},{6,5},{7,4},{8,11},{9,10},{10,... | collective-permute-start | bytes 196616 | tf_op jit(solution)/shard_map/ppermute | solution.py:16

commit v2 on v0

v2 whole, which is shorter than its diff:
```python
import functools

import jax
import jax.numpy as jnp
from jax import lax
from jax.experimental import pallas as pl
from jax.experimental.pallas import tpu as pltpu
from jax.sharding import PartitionSpec as P

masked_low = -1e30
most_direct = 8
depth_block = 256
mebibyte = 2**20

in_hbm = pl.BlockSpec(memory_space=pltpu.MemorySpace.HBM)
in_vmem = pl.BlockSpec(memory_space=pltpu.MemorySpace.VMEM)


def kept_in_hbm(x):
    return pltpu.with_memory_space_constraint(x, pltpu.MemorySpace.HBM)


def kept_in_vmem(x):
    return pltpu.with_memory_space_constraint(x, pltpu.MemorySpace.VMEM)


def is_direct(count):
    return count <= most_direct and count & (count - 1) == 0


def swap(block, axis, distance):
    count = lax.axis_size(axis)
    return lax.ppermute(block, axis, [(i, i ^ distance) for i in range(count)])


def exchange(blocks, axis):
    count = lax.axis_size(axis)
    came = [swap(blocks[d], axis, d) for d in range(count - 1, 0, -1)]
    return [blocks[0]] + came[::-1]


def tree_sum(terms):
    while len(terms) > 1:
        terms = [a + b for a, b in zip(terms[::2], terms[1::2])]
    return terms[0]


def project_kernel(slots_dev, direct, pieces, kv_local, *refs):
    ins, refs = refs[:8], refs[8:]
    slot_hbm, offset_hbm, length_hbm, hidden_hbm, wk_hbm, wv_hbm, wq_hbm, me_ref = ins
    outs, refs = refs[:pieces], refs[pieces:]
    picks_ref, bias_ref, slot, offset, length, hidden, wk, wv, wq, rows, total, small, large = refs
    depth = wq.shape[0]
    blocks = large.shape[0]
    step = depth // blocks
    early = [
        pltpu.make_async_copy(source, target, small.at[i])
        for i, (source, target) in enumerate(
            (
                (slot_hbm, slot),
                (hidden_hbm, hidden),
                (wk_hbm, wk),
                (wv_hbm, wv),
                (offset_hbm, offset),
                (length_hbm, length),
            )
        )
    ]
    spans = [pl.ds(b * step, step) for b in range(blocks)]
    late = [
        pltpu.make_async_copy(wq_hbm.at[span], wq.at[span], large.at[b])
        for b, span in enumerate(spans)
    ]
    for copy in early + late:
        copy.start()

    early[0].wait()
    early[1].wait()
    requests = slot.shape[1]
    place = lax.broadcasted_iota(jnp.int32, (requests, requests), 0)
    if direct:
        me = me_ref[0]
        slot_at = (me ^ (place // slots_dev)) * slots_dev + place % slots_dev
    else:
        slot_at = place
    picks = (slot_at == slot[...]).astype(jnp.float32).astype(jnp.bfloat16)
    picks_ref[...] = picks
    rows[...] = jnp.dot(picks, hidden[...], preferred_element_type=jnp.float32).astype(jnp.bfloat16)

    query_cols, key_cols = wq.shape[1], wk.shape[1]
    early[2].wait()
    total[:, query_cols : query_cols + key_cols] = jnp.dot(
        rows[...], wk[...], preferred_element_type=jnp.float32
    )
    early[3].wait()
    total[:, query_cols + key_cols :] = jnp.dot(
        rows[...], wv[...], preferred_element_type=jnp.float32
    )

    early[4].wait()
    early[5].wait()
    slots, places = bias_ref.shape
    window = places // kv_local
    position = lax.broadcasted_iota(jnp.int32, (1, places), 1) // kv_local
    for s in range(slots):
        gap = offset[s] - position
        distance = jnp.where(gap < 0, gap + window, gap)
        usable = (distance > 0) & (distance < length[s])
        bias_ref[s : s + 1, :] = jnp.where(usable, 0.0, masked_low)

    for b, span in enumerate(spans):
        late[b].wait()
        part = jnp.dot(rows[:, span], wq[span, :], preferred_element_type=jnp.float32)
        if b == 0:
            total[:, :query_cols] = part
        else:
            total[:, :query_cols] += part
    size = requests // pieces
    for d, out in enumerate(outs):
        out[...] = total[d * size : (d + 1) * size, :]


def project(me, slot_of, offset, length, hidden, w_key, w_value, w_query, cache, direct, pieces):
    requests = slot_of.shape[0]
    slots, places = cache.shape[0], cache.shape[1] * cache.shape[2]
    depth, query_cols = w_query.shape
    cols = query_cols + w_key.shape[1] + w_value.shape[1]
    blocks = max(1, depth // depth_block)
    found = pl.pallas_call(
        functools.partial(project_kernel, slots, direct, pieces, cache.shape[2]),
        out_shape=[
            pltpu.VMEM((requests // pieces, cols), jnp.float32) for _ in range(pieces)
        ]
        + [pltpu.VMEM((requests, requests), jnp.bfloat16), pltpu.VMEM((slots, places), jnp.float32)],
        in_specs=[in_hbm] * 7 + [pl.BlockSpec(memory_space=pltpu.MemorySpace.SMEM)],
        out_specs=[in_vmem] * (pieces + 2),
        scratch_shapes=[
            pltpu.VMEM((1, requests), jnp.int32),
            pltpu.SMEM(offset.shape, jnp.int32),
            pltpu.SMEM(length.shape, jnp.int32),
            pltpu.VMEM(hidden.shape, jnp.bfloat16),
            pltpu.VMEM(w_key.shape, jnp.bfloat16),
            pltpu.VMEM(w_value.shape, jnp.bfloat16),
            pltpu.VMEM(w_query.shape, jnp.bfloat16),
            pltpu.VMEM(hidden.shape, jnp.bfloat16),
            pltpu.VMEM((requests, cols), jnp.float32),
            pltpu.SemaphoreType.DMA((6,)),
            pltpu.SemaphoreType.DMA((blocks,)),
        ],
        compiler_params=pltpu.CompilerParams(vmem_limit_bytes=24 * mebibyte),
        cost_estimate=pl.CostEstimate(
            flops=2 * requests * depth * cols, bytes_accessed=2 * depth * cols, transcendentals=0
        ),
    )(
        *[
            kept_in_hbm(x)
            for x in (slot_of.reshape(1, -1), offset, length, hidden, w_key, w_value, w_query)
        ],
        me.reshape(1),
    )
    return found[:pieces], found[pieces], found[pieces + 1]


def fetch_kernel(spans, count, *refs):
    sources, targets, sems = refs[:count], refs[-1 - len(spans) : -1], refs[-1]
    copies = []
    for (which, first, size, cuts), target in zip(spans, targets):
        for c in range(cuts):
            part = size // cuts
            copies.append(
                pltpu.make_async_copy(
                    sources[which].at[pl.ds(first + c * part, part)],
                    target.at[pl.ds(c * part, part)],
                    sems.at[len(copies)],
                )
            )
    for copy in copies:
        copy.start()
    for copy in copies:
        copy.wait()


def fetch(sources, spans, after):
    size = sum(2 * n * sources[w][0].size for w, _, n, _ in spans)
    return pl.pallas_call(
        functools.partial(fetch_kernel, spans, len(sources)),
        out_shape=[pltpu.VMEM((n,) + sources[w].shape[1:], sources[w].dtype) for w, _, n, _ in spans],
        in_specs=[in_hbm] * len(sources) + [in_vmem],
        out_specs=[in_vmem] * len(spans),
        scratch_shapes=[pltpu.SemaphoreType.DMA((sum(c for *_, c in spans),))],
        compiler_params=pltpu.CompilerParams(vmem_limit_bytes=24 * mebibyte),
        cost_estimate=pl.CostEstimate(flops=0, bytes_accessed=size, transcendentals=0),
    )(*[kept_in_hbm(x) for x in sources], kept_in_vmem(after))


def attend_kernel(group, parts_count, kv_local, *refs):
    parts, refs = refs[:parts_count], refs[parts_count:]
    keys, values, bias, heads_ref, keys_ref, values_ref, query_rows, mixed_rows = refs
    slots, places, head_dim = keys.shape
    rows = kv_local * group
    query_cols, key_cols = rows * head_dim, kv_local * head_dim
    fresh = tree_sum([part[...] for part in parts]).astype(jnp.bfloat16)
    keys_ref[...] = fresh[:, query_cols : query_cols + key_cols]
    values_ref[...] = fresh[:, query_cols + key_cols :]
    fresh = fresh.astype(jnp.float32)
    for h in range(rows):
        query_rows[pl.ds(h, slots, stride=rows), :] = fresh[:, h * head_dim : (h + 1) * head_dim]
    scale = 1.0 / jnp.sqrt(jnp.float32(head_dim))
    row_kv = lax.broadcasted_iota(jnp.int32, (rows, 1), 0) // group
    col_kv = lax.broadcasted_iota(jnp.int32, (1, places), 1) % kv_local
    own_head = row_kv == col_kv

    def spread_new(s, first):
        out = fresh[s : s + 1, first : first + head_dim]
        for k in range(1, kv_local):
            left = first + k * head_dim
            out = jnp.where(row_kv == k, fresh[s : s + 1, left : left + head_dim], out)
        return out

    for s in range(slots):
        query = query_rows[s * rows : (s + 1) * rows, :]
        scores = lax.dot_general(
            query.astype(jnp.bfloat16),
            keys[s],
            (((1,), (1,)), ((), ())),
            preferred_element_type=jnp.float32,
        )
        usable = own_head & (bias[s : s + 1, :] == 0.0)
        masked = jnp.where(usable, scores * scale, masked_low)
        latest = jnp.sum(query * spread_new(s, query_cols), axis=1, keepdims=True) * scale
        top = jnp.maximum(jnp.max(masked, axis=1, keepdims=True), latest)
        spread = jnp.exp(masked - top)
        own = jnp.exp(latest - top)
        total = jnp.sum(spread, axis=1, keepdims=True) + own
        weights = (spread / total).astype(jnp.bfloat16)
        own_weight = (own / total).astype(jnp.bfloat16).astype(jnp.float32)
        mixed = jnp.dot(weights, values[s], preferred_element_type=jnp.float32)
        mixed_rows[s * rows : (s + 1) * rows, :] = mixed + own_weight * spread_new(
            s, query_cols + key_cols
        )
    for h in range(rows):
        heads_ref[:, h * head_dim : (h + 1) * head_dim] = mixed_rows[
            pl.ds(h, slots, stride=rows), :
        ].astype(jnp.bfloat16)


def attend(parts, keys, values, bias, kv_local, query_cols):
    slots, places, head_dim = keys.shape
    rows = query_cols // head_dim
    key_cols = kv_local * head_dim
    return pl.pallas_call(
        functools.partial(attend_kernel, rows // kv_local, len(parts), kv_local),
        out_shape=[
            pltpu.VMEM((slots, query_cols), jnp.bfloat16),
            jax.ShapeDtypeStruct((slots, key_cols), jnp.bfloat16),
            jax.ShapeDtypeStruct((slots, key_cols), jnp.bfloat16),
        ],
        in_specs=[in_vmem] * (len(parts) + 3),
        out_specs=[in_vmem] * 3,
        scratch_shapes=[
            pltpu.VMEM((slots * rows, head_dim), jnp.float32),
            pltpu.VMEM((slots * rows, head_dim), jnp.float32),
        ],
        compiler_params=pltpu.CompilerParams(vmem_limit_bytes=24 * mebibyte),
        cost_estimate=pl.CostEstimate(
            flops=4 * slots * rows * places * head_dim,
            bytes_accessed=4 * slots * places * head_dim,
            transcendentals=slots * rows * places,
        ),
    )(*[kept_in_vmem(x) for x in (*parts, keys, values, bias)])


def output_kernel(heads_count, picks_ref, *refs):
    heads, weights, out_ref = refs[:heads_count], refs[heads_count:-1], refs[-1]
    stacked = jnp.concatenate([h[...].astype(jnp.float32) for h in heads], axis=0)
    rows = lax.dot_general(
        picks_ref[...],
        stacked.astype(jnp.bfloat16),
        (((0,), (0,)), ((), ())),
        preferred_element_type=jnp.float32,
    ).astype(jnp.bfloat16)
    found, first = None, 0
    for weight in weights:
        last = first + weight.shape[0]
        part = jnp.dot(rows[:, first:last], weight[...], preferred_element_type=jnp.float32)
        found = part if found is None else found + part
        first = last
    out_ref[...] = found.astype(out_ref.dtype)


def project_out(picks, heads, weights, dtype):
    requests = picks.shape[0]
    cols = weights[0].shape[1]
    size = sum(w.size for w in weights)
    return pl.pallas_call(
        functools.partial(output_kernel, len(heads)),
        out_shape=pltpu.VMEM((requests, cols), dtype),
        in_specs=[in_vmem] * (1 + len(heads) + len(weights)),
        out_specs=in_vmem,
        compiler_params=pltpu.CompilerParams(vmem_limit_bytes=24 * mebibyte),
        cost_estimate=pl.CostEstimate(
            flops=2 * requests * size, bytes_accessed=2 * size, transcendentals=0
        ),
    )(*[kept_in_vmem(x) for x in (picks, *heads, *weights)])


def per_device(
    hidden,
    w_query,
    w_key,
    w_value,
    w_out,
    key_cache,
    value_cache,
    cycle_offset,
    valid_length,
    slot_of,
):
    slots, window, kv_local, head_dim = key_cache.shape
    wide = lax.axis_size("wide")
    direct_wide = is_direct(wide)
    me = lax.axis_index("wide").astype(jnp.int32)
    parts, picks, bias = project(
        me,
        slot_of,
        cycle_offset,
        valid_length,
        hidden,
        w_key,
        w_value,
        w_query,
        key_cache,
        direct_wide,
        wide if direct_wide else 1,
    )
    keys = key_cache.reshape(slots, window * kv_local, head_dim)
    values = value_cache.reshape(slots, window * kv_local, head_dim)
    rows_out = w_out.shape[0]
    cut = rows_out // 4
    keys, values, w_first = fetch(
        [keys, values, w_out], ((0, 0, slots, 2), (1, 0, slots, 2), (2, 0, cut, 2)), bias
    )
    if direct_wide:
        parts = exchange(parts, "wide")
    else:
        parts = [lax.psum_scatter(parts[0], "wide", scatter_dimension=0, tiled=True)]
    heads, keys_out, values_out = attend(parts, keys, values, bias, kv_local, w_query.shape[1])
    (w_rest,) = fetch([w_out], ((0, cut, rows_out - cut, 6),), picks)
    if direct_wide:
        heads = exchange([heads] * wide, "wide")
    else:
        heads = [lax.all_gather(heads, "wide", axis=0, tiled=True)]
    narrow = lax.axis_size("narrow")
    direct_narrow = is_direct(narrow)
    sent = project_out(
        picks, heads, [w_first, w_rest], jnp.bfloat16 if direct_narrow else jnp.float32
    )
    if direct_narrow:
        attn_out = tree_sum([t.astype(jnp.float32) for t in exchange([sent] * narrow, "narrow")])
    else:
        attn_out = lax.psum(sent, "narrow")
    return (attn_out.astype(jnp.bfloat16), keys_out, values_out)


def solution(mesh):
    placed = (
        P("groups", "wide"),
        P("wide", "narrow"),
        P("wide", "narrow"),
        P("wide", "narrow"),
        P("narrow", "wide"),
        P(("groups", "wide"), None, "narrow", None),
        P(("groups", "wide"), None, "narrow", None),
        P(("groups", "wide")),
        P(("groups", "wide")),
        P("groups"),
    )
    return jax.shard_map(
        per_device,
        mesh=mesh,
        in_specs=placed,
        out_specs=(
            P("groups", "wide"),
            P(("groups", "wide"), "narrow"),
            P(("groups", "wide"), "narrow"),
        ),
        check_vma=False,
    )
```

time: 66.8 us -> 34.7 us (0.52)
  blocking collectives: 48.9 us -> 0 us
  Pallas kernels: 0 us -> 14 us
  starting transfers between devices: 0 us -> 11.9 us
  matrix products: 10.9 us -> 0 us
  waiting for transfers between devices: 0 us -> 7.18 us
  local copies, waits for them, and re-layouts: 4.13 us -> 0 us
  between operations: 1.5 us -> 0.7 us
    unnamed x1 -> x0, blocking collectives: 23.7 us -> none
    pallas_call x0 -> x5, Pallas kernels: none -> 14 us  [the longest x2 5.39 us: fetch(): pl.pallas_call(functools.partial(fetch_kernel, spans, len(sources)), out_...]
    all_gather x1 -> x0, blocking collectives: 13.2 us -> none  [per_device(): lax.all_gather(heads, 'wide', axis=0, tiled=True)]
    psum x1 -> x0, blocking collectives: 12 us -> none  [per_device(): attn_out = lax.psum(request_out, 'narrow').astype(jnp.bfloat16)]
    ppermute x0 -> x9, starting transfers between devices: none -> 11.9 us  [swap(): return lax.ppermute(block, axis, [(i, i ^ distance) for i in range(count)])]
    dot_general x7 -> x0, matrix products: 10.9 us -> none  [the longest x1 4.72 us: per_device(): jnp.dot(rows, w_query, preferred_element_type=jnp.float32)]
    ppermute x0 -> x9, waiting for transfers between devices: none -> 7.18 us  [swap(): return lax.ppermute(block, axis, [(i, i ^ distance) for i in range(count)])]
    gather x3 -> x0, local copies, waits for them, and re-layouts: 2.77 us -> none  [the longest x1 1.51 us: per_device(): hidden[order[jnp.arange(slots_dev * lax.axis_size('wide'), dtype=jnp.int3...]
  transfers between devices with their start and end apart: 0 -> 9, of which waited for: 0 -> 4; matrix products, arithmetic and copies ran while one was open for 0% -> 0% of each run, Pallas kernels for 0% -> 16%
where the time goes in v2:
time: 34.7 us; the launch traced here: 34.5 us
  Pallas kernels  14 us (40%)
  starting transfers between devices  11.9 us (34%)
  waiting for transfers between devices  7.18 us (21%)
  between operations  0.7 us (2%)
  other arithmetic  0.67 us (2%)
    ppermute x9, starting transfers between devices, swap(): return lax.ppermute(block, axis, [(i, i ^ distance) for i in range(count)])  11.9 us
    ppermute x9, waiting for transfers between devices, swap(): return lax.ppermute(block, axis, [(i, i ^ distance) for i in range(count)])  7.18 us
    pallas_call x2, Pallas kernels, fetch(): pl.pallas_call(functools.partial(fetch_kernel, spans, len(sources)), out_...  5.39 us
    pallas_call x1, Pallas kernels, project(): pl.pallas_call(functools.partial(project_kernel, slots, direct, pieces, c...  4.97 us
    pallas_call x1, Pallas kernels, attend(): pl.pallas_call(functools.partial(attend_kernel, rows // kv_local, len(par...  2.34 us
    pallas_call x1, Pallas kernels, project_out(): pl.pallas_call(functools.partial(output_kernel, len(heads)), out_shape=pl...  1.34 us
  transfers between devices with their start and end apart: 9, of which 4 were waited for; matrix products, arithmetic and copies ran while one was open for 0% of the time, Pallas kernels for 16%

profile of v2, /device:TPU:0, one launch (start us, length us, event | category | flops | bytes accessed | tf_op | source)
XLA Modules:
  0.0 34.5 jit_solution(300114047691691413)
XLA Ops:
  0.6 5.0 %shard_map.121 = (f32[4,2560]{1,0:T(4,128)S(1)}, f32[4,2560]{1,0:T(4,128)S(1)}, f32[4,2560]{1,0:T(4,128)S(1)}, f32[4,2560]{1,0:T(4,128)S(1)}, bf16[16,16]{1,0:T(8,128)(2,1)S(1)}, /*index=5*/f32[4,1536]{1,0:T(4,128)S(1)}) custom-call(s32[1,16]{1,0:T(1,128)} %bitcast.6, s32[4]{0:T(128)} %refs_1_.1, s32[4]{0:T(128)} %refs_2_.2, bf16[16,2048]{1,0:T(8,128)(2,1)} %refs_3_.1, ...), custom_call_target="tpu_custom_call" | custom-call | flops 167772160 | bytes 10485760 | tf_op jit(solution)/shard_map/pallas_call | solution.py:129
  5.6 3.1 %collective-permute-start = (f32[4,2560]{1,0:T(4,128)S(1)}, f32[4,2560]{1,0:T(4,128)S(1)}, u32[]{:S(2)}, u32[]{:S(2)}) collective-permute-start(f32[4,2560]{1,0:T(4,128)S(1)} %get-tuple-element.17), channel_id=1, source_target_pairs={{0,4},{4,0},{8,12},{12,8},{1,5},{5,1},{9,13},{13,9},{2,6},{6,2},{1... | collective-permute-start | bytes 122888 | tf_op jit(solution)/shard_map/ppermute | solution.py:33
  8.7 2.6 %collective-permute-start.1 = (f32[4,2560]{1,0:T(4,128)S(1)}, f32[4,2560]{1,0:T(4,128)S(1)}, u32[]{:S(2)}, u32[]{:S(2)}) collective-permute-start(f32[4,2560]{1,0:T(4,128)S(1)} %get-tuple-element.18), channel_id=1, source_target_pairs={{0,8},{4,12},{8,0},{12,4},{1,9},{5,13},{9,1},{13,5},{2,10},{6,14},... | collective-permute-start | bytes 122888 | tf_op jit(solution)/shard_map/ppermute | solution.py:33
  11.3 0.0 collective-permute-start.2
  11.3 2.5 %shard_map.122 = (bf16[4,1536,128]{2,1,0:T(8,128)(2,1)S(1)}, bf16[4,1536,128]{2,1,0:T(8,128)(2,1)S(1)}, bf16[512,2048]{1,0:T(8,128)(2,1)S(1)}) custom-call(bf16[4,1536,128]{2,1,0:T(8,128)(2,1)} %bitcast.4, bf16[4,1536,128]{2,1,0:T(8,128)(2,1)} %bitcast.5, bf16[2048,2048]{1,0:T(8,128)(2,1)} %refs_0_.1, f32[4,1536]{1,0:T(4,128)S(1)} %get-tuple-element.20.refs_3_.refs_6_), custom_call_target="tpu_custom_call" | custom-call | bytes 5242880 | tf_op jit(solution)/shard_map/pallas_call | solution.py:185
  13.8 0.0 collective-permute-done.refs_1_
  13.9 0.5 %collective-permute-done.1.refs_2_ = f32[4,2560]{1,0:T(4,128)S(1)} collective-permute-done((f32[4,2560]{1,0:T(4,128)S(1)}, f32[4,2560]{1,0:T(4,128)S(1)}, u32[]{:S(2)}, u32[]{:S(2)}) %collective-permute-start.1) | collective-permute-done | bytes 40992 | tf_op jit(solution)/shard_map/ppermute | solution.py:33
  14.4 2.7 %collective-permute-done.2.refs_3_ = f32[4,2560]{1,0:T(4,128)S(1)} collective-permute-done((f32[4,2560]{1,0:T(4,128)S(1)}, f32[4,2560]{1,0:T(4,128)S(1)}, u32[]{:S(2)}, u32[]{:S(2)}) %collective-permute-start.2) | collective-permute-done | bytes 40992 | tf_op jit(solution)/shard_map/ppermute | solution.py:33
  17.1 2.3 %shard_map.123 = (bf16[4,2048]{1,0:T(4,128)(2,1)S(1)}, bf16[4,256]{1,0:T(4,128)(2,1)}, bf16[4,256]{1,0:T(4,128)(2,1)}) custom-call(f32[4,2560]{1,0:T(4,128)S(1)} %get-tuple-element.16.refs_0_, f32[4,2560]{1,0:T(4,128)S(1)} %collective-permute-done.refs_1_, f32[4,2560]{1,0:T(4,128)S(1)} %collective-permute-done.1.refs_2_, ...), custom_call_target="tpu_custom_call" | custom-call | flops 50331648 | bytes 3145728 | tf_op jit(solution)/shard_map/pallas_call | solution.py:251
  19.4 0.6 %collective-permute-start.5 = (bf16[4,2048]{1,0:T(4,128)(2,1)S(1)}, bf16[4,2048]{1,0:T(4,128)(2,1)S(1)}, u32[]{:S(2)}, u32[]{:S(2)}) collective-permute-start(bf16[4,2048]{1,0:T(4,128)(2,1)S(1)} %get-tuple-element.23.refs_0_), channel_id=1, source_target_pairs={{0,12},{4,8},{8,4},{12,0},{1,13},{5,9},{9,5},{13,1},{2,14},{6,10},... | collective-permute-start | bytes 49160 | tf_op jit(solution)/shard_map/ppermute | solution.py:33
  20.0 0.0 collective-permute-start.4
  20.0 3.8 %collective-permute-start.3 = (bf16[4,2048]{1,0:T(4,128)(2,1)S(1)}, bf16[4,2048]{1,0:T(4,128)(2,1)S(1)}, u32[]{:S(2)}, u32[]{:S(2)}) collective-permute-start(bf16[4,2048]{1,0:T(4,128)(2,1)S(1)} %get-tuple-element.23.refs_0_), channel_id=1, source_target_pairs={{0,4},{4,0},{8,12},{12,8},{1,5},{5,1},{9,13},{13,9},{2,6},{6,2},{1... | collective-permute-start | bytes 49160 | tf_op jit(solution)/shard_map/ppermute | solution.py:33
  23.8 2.9 %shard_map.124.refs_5_ = bf16[1536,2048]{1,0:T(8,128)(2,1)S(1)} custom-call(bf16[2048,2048]{1,0:T(8,128)(2,1)} %refs_0_.1, bf16[16,16]{1,0:T(8,128)(2,1)S(1)} %get-tuple-element.15.refs_1_.picks_ref), custom_call_target="tpu_custom_call" | custom-call | bytes 6291456 | tf_op jit(solution)/shard_map/pallas_call | solution.py:185
  26.7 0.0 collective-permute-done.5.refs_3_
  26.7 0.0 collective-permute-done.4.refs_2_
  26.7 0.0 collective-permute-done.3.refs_1_
  26.7 1.3 %shard_map.125 = bf16[16,2048]{1,0:T(8,128)(2,1)S(1)} custom-call(bf16[16,16]{1,0:T(8,128)(2,1)S(1)} %get-tuple-element.15.refs_1_.picks_ref, bf16[4,2048]{1,0:T(4,128)(2,1)S(1)} %get-tuple-element.23.refs_0_, bf16[4,2048]{1,0:T(4,128)(2,1)S(1)} %collective-permute-done.3.refs_1_, bf16[4,2048]{1,0:T(4,128)(2,1)S(1)} %collective-permute-done.4.refs_2_, ...), custom_call_target="tpu_custom_call" | custom-call | flops 134217728 | bytes 8388608 | tf_op jit(solution)/shard_map/pallas_call | solution.py:295
  28.1 0.0 collective-permute-start.8
  28.1 1.6 %collective-permute-start.7 = (bf16[16,2048]{1,0:T(8,128)(2,1)S(1)}, bf16[16,2048]{1,0:T(8,128)(2,1)S(1)}, u32[]{:S(2)}, u32[]{:S(2)}) collective-permute-start(bf16[16,2048]{1,0:T(8,128)(2,1)S(1)} %shard_map.125), channel_id=1, source_target_pairs={{0,2},{1,3},{2,0},{3,1},{4,6},{5,7},{6,4},{7,5},{8,10},{9,11},{10,... | collective-permute-start | bytes 196616 | tf_op jit(solution)/shard_map/ppermute | solution.py:33
  29.6 0.3 collective-permute-start.6
  29.9 2.5 %collective-permute-done.8 = bf16[16,2048]{1,0:T(8,128)(2,1)S(1)} collective-permute-done((bf16[16,2048]{1,0:T(8,128)(2,1)S(1)}, bf16[16,2048]{1,0:T(8,128)(2,1)S(1)}, u32[]{:S(2)}, u32[]{:S(2)}) %collective-permute-start.8) | collective-permute-done | bytes 65568 | tf_op jit(solution)/shard_map/ppermute | solution.py:33
  32.4 1.4 %collective-permute-done.7 = bf16[16,2048]{1,0:T(8,128)(2,1)S(1)} collective-permute-done((bf16[16,2048]{1,0:T(8,128)(2,1)S(1)}, bf16[16,2048]{1,0:T(8,128)(2,1)S(1)}, u32[]{:S(2)}, u32[]{:S(2)}) %collective-permute-start.7) | collective-permute-done | bytes 65568 | tf_op jit(solution)/shard_map/ppermute | solution.py:33
  33.9 0.0 collective-permute-done.6
  33.9 0.7 %add_convert_fusion = bf16[16,2048]{1,0:T(8,128)(2,1)} fusion(bf16[16,2048]{1,0:T(8,128)(2,1)S(1)} %collective-permute-done.8, bf16[16,2048]{1,0:T(8,128)(2,1)S(1)} %collective-permute-done.7, bf16[16,2048]{1,0:T(8,128)(2,1)S(1)} %collective-permute-done.6, bf16[16,2048]{1,0:T(8,128)(2,1)S(1)} %shard_map.125), kind=kLoop, calls=%fused_computation | loop fusion | flops 262144 | bytes 327680 | tf_op jit(solution)/shard_map/convert_element_type | solution.py:362
Async XLA Ops:
  5.6 8.2 %collective-permute-start = (f32[4,2560]{1,0:T(4,128)S(1)}, f32[4,2560]{1,0:T(4,128)S(1)}, u32[]{:S(2)}, u32[]{:S(2)}) collective-permute-start(f32[4,2560]{1,0:T(4,128)S(1)} %get-tuple-element.17), channel_id=1, source_target_pairs={{0,4},{4,0},{8,12},{12,8},{1,5},{5,1},{9,13},{13,9},{2,6},{6,2},{1... | collective-permute-start | bytes 122888 | tf_op jit(solution)/shard_map/ppermute | solution.py:33
  8.7 5.7 %collective-permute-start.1 = (f32[4,2560]{1,0:T(4,128)S(1)}, f32[4,2560]{1,0:T(4,128)S(1)}, u32[]{:S(2)}, u32[]{:S(2)}) collective-permute-start(f32[4,2560]{1,0:T(4,128)S(1)} %get-tuple-element.18), channel_id=1, source_target_pairs={{0,8},{4,12},{8,0},{12,4},{1,9},{5,13},{9,1},{13,5},{2,10},{6,14},... | collective-permute-start | bytes 122888 | tf_op jit(solution)/shard_map/ppermute | solution.py:33
  11.3 5.8 %collective-permute-start.2 = (f32[4,2560]{1,0:T(4,128)S(1)}, f32[4,2560]{1,0:T(4,128)S(1)}, u32[]{:S(2)}, u32[]{:S(2)}) collective-permute-start(f32[4,2560]{1,0:T(4,128)S(1)} %get-tuple-element.19), channel_id=1, source_target_pairs={{0,12},{4,8},{8,4},{12,0},{1,13},{5,9},{9,5},{13,1},{2,14},{6,10},... | collective-permute-start | bytes 122888 | tf_op jit(solution)/shard_map/ppermute | solution.py:33
  19.4 7.3 %collective-permute-start.5 = (bf16[4,2048]{1,0:T(4,128)(2,1)S(1)}, bf16[4,2048]{1,0:T(4,128)(2,1)S(1)}, u32[]{:S(2)}, u32[]{:S(2)}) collective-permute-start(bf16[4,2048]{1,0:T(4,128)(2,1)S(1)} %get-tuple-element.23.refs_0_), channel_id=1, source_target_pairs={{0,12},{4,8},{8,4},{12,0},{1,13},{5,9},{9,5},{13,1},{2,14},{6,10},... | collective-permute-start | bytes 49160 | tf_op jit(solution)/shard_map/ppermute | solution.py:33
  20.0 6.7 %collective-permute-start.4 = (bf16[4,2048]{1,0:T(4,128)(2,1)S(1)}, bf16[4,2048]{1,0:T(4,128)(2,1)S(1)}, u32[]{:S(2)}, u32[]{:S(2)}) collective-permute-start(bf16[4,2048]{1,0:T(4,128)(2,1)S(1)} %get-tuple-element.23.refs_0_), channel_id=1, source_target_pairs={{0,8},{4,12},{8,0},{12,4},{1,9},{5,13},{9,1},{13,5},{2,10},{6,14},... | collective-permute-start | bytes 49160 | tf_op jit(solution)/shard_map/ppermute | solution.py:33
  20.0 6.7 %collective-permute-start.3 = (bf16[4,2048]{1,0:T(4,128)(2,1)S(1)}, bf16[4,2048]{1,0:T(4,128)(2,1)S(1)}, u32[]{:S(2)}, u32[]{:S(2)}) collective-permute-start(bf16[4,2048]{1,0:T(4,128)(2,1)S(1)} %get-tuple-element.23.refs_0_), channel_id=1, source_target_pairs={{0,4},{4,0},{8,12},{12,8},{1,5},{5,1},{9,13},{13,9},{2,6},{6,2},{1... | collective-permute-start | bytes 49160 | tf_op jit(solution)/shard_map/ppermute | solution.py:33
  28.1 4.4 %collective-permute-start.8 = (bf16[16,2048]{1,0:T(8,128)(2,1)S(1)}, bf16[16,2048]{1,0:T(8,128)(2,1)S(1)}, u32[]{:S(2)}, u32[]{:S(2)}) collective-permute-start(bf16[16,2048]{1,0:T(8,128)(2,1)S(1)} %shard_map.125), channel_id=1, source_target_pairs={{0,3},{1,2},{2,1},{3,0},{4,7},{5,6},{6,5},{7,4},{8,11},{9,10},{10,... | collective-permute-start | bytes 196616 | tf_op jit(solution)/shard_map/ppermute | solution.py:33
  28.1 5.8 %collective-permute-start.7 = (bf16[16,2048]{1,0:T(8,128)(2,1)S(1)}, bf16[16,2048]{1,0:T(8,128)(2,1)S(1)}, u32[]{:S(2)}, u32[]{:S(2)}) collective-permute-start(bf16[16,2048]{1,0:T(8,128)(2,1)S(1)} %shard_map.125), channel_id=1, source_target_pairs={{0,2},{1,3},{2,0},{3,1},{4,6},{5,7},{6,4},{7,5},{8,10},{9,11},{10,... | collective-permute-start | bytes 196616 | tf_op jit(solution)/shard_map/ppermute | solution.py:33
  29.6 4.3 %collective-permute-start.6 = (bf16[16,2048]{1,0:T(8,128)(2,1)S(1)}, bf16[16,2048]{1,0:T(8,128)(2,1)S(1)}, u32[]{:S(2)}, u32[]{:S(2)}) collective-permute-start(bf16[16,2048]{1,0:T(8,128)(2,1)S(1)} %shard_map.125), channel_id=1, source_target_pairs={{0,1},{1,0},{2,3},{3,2},{4,5},{5,4},{6,7},{7,6},{8,9},{9,8},{10,11... | collective-permute-start | bytes 196616 | tf_op jit(solution)/shard_map/ppermute | solution.py:33

commit v3 on v2

v3 whole, which is shorter than its diff:
```python
import functools

import jax
import jax.numpy as jnp
from jax import lax
from jax.experimental import pallas as pl
from jax.experimental.pallas import tpu as pltpu
from jax.sharding import PartitionSpec as P

masked_low = -1e30
most_direct = 8
depth_block = 512
mebibyte = 2**20

in_hbm = pl.BlockSpec(memory_space=pltpu.MemorySpace.HBM)
in_vmem = pl.BlockSpec(memory_space=pltpu.MemorySpace.VMEM)


def kept_in_hbm(x):
    return pltpu.with_memory_space_constraint(x, pltpu.MemorySpace.HBM)


def kept_in_vmem(x):
    return pltpu.with_memory_space_constraint(x, pltpu.MemorySpace.VMEM)


def is_direct(count):
    return count <= most_direct and count & (count - 1) == 0


def swap(block, axis, distance):
    count = lax.axis_size(axis)
    return lax.ppermute(block, axis, [(i, i ^ distance) for i in range(count)])


def exchange(blocks, axis):
    count = lax.axis_size(axis)
    came = [swap(blocks[d], axis, d) for d in range(count - 1, 0, -1)]
    return [blocks[0]] + came[::-1]


def tree_sum(terms):
    while len(terms) > 1:
        terms = [a + b for a, b in zip(terms[::2], terms[1::2])]
    return terms[0]


def project_kernel(slots_dev, direct, pieces, kv_local, *refs):
    ins, refs = refs[:8], refs[8:]
    slot_hbm, offset_hbm, length_hbm, hidden_hbm, wk_hbm, wv_hbm, wq_hbm, me_ref = ins
    outs, refs = refs[:pieces], refs[pieces:]
    picks_ref, bias_ref, slot, offset, length, hidden, wk, wv, wq, rows, total, small, large = refs
    depth = wq.shape[0]
    blocks = large.shape[0] - 2
    step = depth // blocks
    early = [
        pltpu.make_async_copy(source, target, small.at[i])
        for i, (source, target) in enumerate(
            ((slot_hbm, slot), (hidden_hbm, hidden), (offset_hbm, offset), (length_hbm, length))
        )
    ]
    query_cols, key_cols = wq.shape[1], wk.shape[1]
    plan = [
        (wk_hbm, wk, 0, depth, query_cols),
        (wv_hbm, wv, 0, depth, query_cols + key_cols),
    ] + [(wq_hbm, wq, b * step, step, 0) for b in range(blocks)]
    late = [
        pltpu.make_async_copy(
            source.at[pl.ds(first, size)], target.at[pl.ds(first, size)], large.at[i]
        )
        for i, (source, target, first, size, _) in enumerate(plan)
    ]
    for copy in early + late:
        copy.start()

    early[0].wait()
    early[1].wait()
    requests = slot.shape[1]
    place = lax.broadcasted_iota(jnp.int32, (requests, requests), 0)
    if direct:
        me = me_ref[0]
        slot_at = (me ^ (place // slots_dev)) * slots_dev + place % slots_dev
    else:
        slot_at = place
    picks = (slot_at == slot[...]).astype(jnp.float32).astype(jnp.bfloat16)
    picks_ref[...] = picks
    rows[...] = jnp.dot(picks, hidden[...], preferred_element_type=jnp.float32).astype(jnp.bfloat16)

    early[2].wait()
    early[3].wait()
    slots, places = bias_ref.shape
    window = places // kv_local
    position = lax.broadcasted_iota(jnp.int32, (1, places), 1) // kv_local
    for s in range(slots):
        gap = offset[s] - position
        distance = jnp.where(gap < 0, gap + window, gap)
        usable = (distance > 0) & (distance < length[s])
        bias_ref[s : s + 1, :] = jnp.where(usable, 0.0, masked_low)

    for copy, (_, weight, first, size, left) in zip(late, plan):
        copy.wait()
        span = pl.ds(first, size)
        right = left + weight.shape[1]
        part = jnp.dot(rows[:, span], weight[span, :], preferred_element_type=jnp.float32)
        if first == 0:
            total[:, left:right] = part
        else:
            total[:, left:right] += part
    size = requests // pieces
    for d, out in enumerate(outs[::-1]):
        out[...] = total[d * size : (d + 1) * size, :]


def project(me, slot_of, offset, length, hidden, w_key, w_value, w_query, cache, direct, pieces):
    requests = slot_of.shape[0]
    slots, places = cache.shape[0], cache.shape[1] * cache.shape[2]
    depth, query_cols = w_query.shape
    cols = query_cols + w_key.shape[1] + w_value.shape[1]
    blocks = max(1, depth // depth_block)
    found = pl.pallas_call(
        functools.partial(project_kernel, slots, direct, pieces, cache.shape[2]),
        out_shape=[pltpu.VMEM((requests // pieces, cols), jnp.float32) for _ in range(pieces)]
        + [pltpu.VMEM((requests, requests), jnp.bfloat16), pltpu.VMEM((slots, places), jnp.float32)],
        in_specs=[in_hbm] * 7 + [pl.BlockSpec(memory_space=pltpu.MemorySpace.SMEM)],
        out_specs=[in_vmem] * (pieces + 2),
        scratch_shapes=[
            pltpu.VMEM((1, requests), jnp.int32),
            pltpu.SMEM(offset.shape, jnp.int32),
            pltpu.SMEM(length.shape, jnp.int32),
            pltpu.VMEM(hidden.shape, jnp.bfloat16),
            pltpu.VMEM(w_key.shape, jnp.bfloat16),
            pltpu.VMEM(w_value.shape, jnp.bfloat16),
            pltpu.VMEM(w_query.shape, jnp.bfloat16),
            pltpu.VMEM(hidden.shape, jnp.bfloat16),
            pltpu.VMEM((requests, cols), jnp.float32),
            pltpu.SemaphoreType.DMA((4,)),
            pltpu.SemaphoreType.DMA((blocks + 2,)),
        ],
        compiler_params=pltpu.CompilerParams(vmem_limit_bytes=24 * mebibyte),
        cost_estimate=pl.CostEstimate(
            flops=2 * requests * depth * cols, bytes_accessed=2 * depth * cols, transcendentals=0
        ),
    )(
        *[
            kept_in_hbm(x)
            for x in (slot_of.reshape(1, -1), offset, length, hidden, w_key, w_value, w_query)
        ],
        me.reshape(1),
    )
    return found[:pieces][::-1], found[pieces], found[pieces + 1]


def attend_kernel(group, parts_count, kv_local, *refs):
    parts, refs = refs[:parts_count], refs[parts_count:]
    keys, values, bias, heads_ref, keys_ref, values_ref, query_rows, mixed_rows = refs
    slots, places, head_dim = keys.shape
    rows = kv_local * group
    query_cols, key_cols = rows * head_dim, kv_local * head_dim
    fresh = tree_sum([part[...] for part in parts]).astype(jnp.bfloat16)
    keys_ref[...] = fresh[:, query_cols : query_cols + key_cols]
    values_ref[...] = fresh[:, query_cols + key_cols :]
    fresh = fresh.astype(jnp.float32)
    for h in range(rows):
        query_rows[pl.ds(h, slots, stride=rows), :] = fresh[:, h * head_dim : (h + 1) * head_dim]
    scale = 1.0 / head_dim**0.5
    row_kv = lax.broadcasted_iota(jnp.int32, (rows, 1), 0) // group
    col_kv = lax.broadcasted_iota(jnp.int32, (1, places), 1) % kv_local
    own_head = row_kv == col_kv

    def spread_new(s, first):
        out = fresh[s : s + 1, first : first + head_dim]
        for k in range(1, kv_local):
            left = first + k * head_dim
            out = jnp.where(row_kv == k, fresh[s : s + 1, left : left + head_dim], out)
        return out

    every = range(slots)
    query = [query_rows[s * rows : (s + 1) * rows, :] for s in every]
    scores = [
        lax.dot_general(
            query[s].astype(jnp.bfloat16),
            keys[s],
            (((1,), (1,)), ((), ())),
            preferred_element_type=jnp.float32,
        )
        for s in every
    ]
    latest = [
        jnp.sum(query[s] * spread_new(s, query_cols), axis=1, keepdims=True) for s in every
    ]
    masked = [
        jnp.where(own_head & (bias[s : s + 1, :] == 0.0), scores[s], masked_low) for s in every
    ]
    top = [
        jnp.maximum(jnp.max(masked[s], axis=1, keepdims=True), latest[s]) for s in every
    ]
    spread = [jnp.exp((masked[s] - top[s]) * scale) for s in every]
    own = [jnp.exp((latest[s] - top[s]) * scale) for s in every]
    total = [jnp.sum(spread[s], axis=1, keepdims=True) + own[s] for s in every]
    mixed = [
        jnp.dot(spread[s].astype(jnp.bfloat16), values[s], preferred_element_type=jnp.float32)
        for s in every
    ]
    for s in every:
        mixed_rows[s * rows : (s + 1) * rows, :] = (
            mixed[s] + own[s] * spread_new(s, query_cols + key_cols)
        ) / total[s]
    for h in range(rows):
        heads_ref[:, h * head_dim : (h + 1) * head_dim] = mixed_rows[
            pl.ds(h, slots, stride=rows), :
        ].astype(jnp.bfloat16)


def attend(parts, keys, values, bias, kv_local, query_cols):
    slots, places, head_dim = keys.shape
    rows = query_cols // head_dim
    key_cols = kv_local * head_dim
    return pl.pallas_call(
        functools.partial(attend_kernel, rows // kv_local, len(parts), kv_local),
        out_shape=[
            pltpu.VMEM((slots, query_cols), jnp.bfloat16),
            pltpu.VMEM((slots, key_cols), jnp.bfloat16),
            pltpu.VMEM((slots, key_cols), jnp.bfloat16),
        ],
        in_specs=[in_vmem] * (len(parts) + 3),
        out_specs=[in_vmem] * 3,
        scratch_shapes=[
            pltpu.VMEM((slots * rows, head_dim), jnp.float32),
            pltpu.VMEM((slots * rows, head_dim), jnp.float32),
        ],
        compiler_params=pltpu.CompilerParams(vmem_limit_bytes=24 * mebibyte),
        cost_estimate=pl.CostEstimate(
            flops=4 * slots * rows * places * head_dim,
            bytes_accessed=4 * slots * places * head_dim,
            transcendentals=slots * rows * places,
        ),
    )(*[kept_in_vmem(x) for x in parts], keys, values, kept_in_vmem(bias))


def output_kernel(heads_count, picks_ref, keys_ref, values_ref, *refs):
    heads, weight, refs = refs[:heads_count], refs[heads_count], refs[heads_count + 1 :]
    out_ref, keys_hbm, values_hbm, sems = refs
    copies = [
        pltpu.make_async_copy(keys_ref, keys_hbm, sems.at[0]),
        pltpu.make_async_copy(values_ref, values_hbm, sems.at[1]),
    ]
    for copy in copies:
        copy.start()
    stacked = jnp.concatenate([h[...].astype(jnp.float32) for h in heads], axis=0)
    rows = lax.dot_general(
        picks_ref[...],
        stacked.astype(jnp.bfloat16),
        (((0,), (0,)), ((), ())),
        preferred_element_type=jnp.float32,
    ).astype(jnp.bfloat16)
    out_ref[...] = jnp.dot(rows, weight[...], preferred_element_type=jnp.float32).astype(
        out_ref.dtype
    )
    for copy in copies:
        copy.wait()


def project_out(picks, keys, values, heads, weight, dtype):
    requests = picks.shape[0]
    return pl.pallas_call(
        functools.partial(output_kernel, len(heads)),
        out_shape=[
            pltpu.VMEM((requests, weight.shape[1]), dtype),
            pltpu.MemorySpace.HBM(keys.shape, keys.dtype),
            pltpu.MemorySpace.HBM(values.shape, values.dtype),
        ],
        in_specs=[in_vmem] * (4 + len(heads)),
        out_specs=[in_vmem, in_hbm, in_hbm],
        scratch_shapes=[pltpu.SemaphoreType.DMA((2,))],
        compiler_params=pltpu.CompilerParams(vmem_limit_bytes=24 * mebibyte),
        cost_estimate=pl.CostEstimate(
            flops=2 * requests * weight.size, bytes_accessed=2 * weight.size, transcendentals=0
        ),
    )(*[kept_in_vmem(x) for x in (picks, keys, values, *heads)], weight)


def per_device(
    hidden,
    w_query,
    w_key,
    w_value,
    w_out,
    key_cache,
    value_cache,
    cycle_offset,
    valid_length,
    slot_of,
):
    slots, window, kv_local, head_dim = key_cache.shape
    wide = lax.axis_size("wide")
    direct_wide = is_direct(wide)
    me = lax.axis_index("wide").astype(jnp.int32)
    parts, picks, bias = project(
        me,
        slot_of,
        cycle_offset,
        valid_length,
        hidden,
        w_key,
        w_value,
        w_query,
        key_cache,
        direct_wide,
        wide if direct_wide else 1,
    )
    keys = key_cache.reshape(slots, window * kv_local, head_dim)
    values = value_cache.reshape(slots, window * kv_local, head_dim)
    if direct_wide:
        parts = exchange(parts, "wide")
    else:
        parts = [lax.psum_scatter(parts[0], "wide", scatter_dimension=0, tiled=True)]
    heads, keys_out, values_out = attend(parts[::-1], keys, values, bias, kv_local, w_query.shape[1])
    if direct_wide:
        heads = exchange([heads] * wide, "wide")
    else:
        heads = [lax.all_gather(heads, "wide", axis=0, tiled=True)]
    narrow = lax.axis_size("narrow")
    direct_narrow = is_direct(narrow)
    sent, keys_out, values_out = project_out(
        picks,
        keys_out,
        values_out,
        heads,
        w_out,
        jnp.bfloat16 if direct_narrow else jnp.float32,
    )
    if direct_narrow:
        distance = narrow // 2
        attn_out = sent
        while distance >= 1:
            attn_out = attn_out.astype(jnp.float32) + swap(attn_out, "narrow", distance).astype(jnp.float32)
            distance //= 2
            attn_out = attn_out.astype(jnp.bfloat16)
    else:
        attn_out = lax.psum(sent, "narrow")
    return (attn_out.astype(jnp.bfloat16), keys_out, values_out)


def solution(mesh):
    placed = (
        P("groups", "wide"),
        P("wide", "narrow"),
        P("wide", "narrow"),
        P("wide", "narrow"),
        P("narrow", "wide"),
        P(("groups", "wide"), None, "narrow", None),
        P(("groups", "wide"), None, "narrow", None),
        P(("groups", "wide")),
        P(("groups", "wide")),
        P("groups"),
    )
    return jax.shard_map(
        per_device,
        mesh=mesh,
        in_specs=placed,
        out_specs=(
            P("groups", "wide"),
            P(("groups", "wide"), "narrow"),
            P(("groups", "wide"), "narrow"),
        ),
        check_vma=False,
    )
```

time: 34.7 us -> 30.4 us (0.88)
  Pallas kernels: 14 us -> 6.88 us
  waiting for transfers between devices: 7.18 us -> 10.2 us
    pallas_call x3 -> x1, Pallas kernels: 6.73 us -> 1.37 us  [project_out(): pl.pallas_call(functools.partial(output_kernel, len(heads)), out_shape=[p...]
    ppermute x9 -> x8, waiting for transfers between devices: 7.18 us -> 10.2 us  [swap(): return lax.ppermute(block, axis, [(i, i ^ distance) for i in range(count)])]
    pallas_call x1, Pallas kernels: 2.34 us -> 0.78 us  [attend(): pl.pallas_call(functools.partial(attend_kernel, rows // kv_local, len(par...]
    ppermute x9 -> x8, starting transfers between devices: 11.9 us -> 11.8 us  [swap(): return lax.ppermute(block, axis, [(i, i ^ distance) for i in range(count)])]
  transfers between devices with their start and end apart: 9 -> 8, of which waited for: 4 -> 6; matrix products, arithmetic and copies ran while one was open for 0% -> 0% of each run, Pallas kernels for 16% -> 0%
where the time goes in v3:
time: 30.4 us; the launch traced here: 30.3 us
  starting transfers between devices  11.8 us (39%)
  waiting for transfers between devices  10.2 us (34%)
  Pallas kernels  6.88 us (23%)
  between operations  0.71 us (2%)
  other arithmetic  0.67 us (2%)
    ppermute x8, starting transfers between devices, swap(): return lax.ppermute(block, axis, [(i, i ^ distance) for i in range(count)])  11.8 us
    ppermute x8, waiting for transfers between devices, swap(): return lax.ppermute(block, axis, [(i, i ^ distance) for i in range(count)])  10.2 us
    pallas_call x1, Pallas kernels, project(): pl.pallas_call(functools.partial(project_kernel, slots, direct, pieces, c...  4.73 us
    pallas_call x1, Pallas kernels, project_out(): pl.pallas_call(functools.partial(output_kernel, len(heads)), out_shape=[p...  1.37 us
    pallas_call x1, Pallas kernels, attend(): pl.pallas_call(functools.partial(attend_kernel, rows // kv_local, len(par...  0.78 us
    convert_element_type x2, other arithmetic, per_device(): attn_out = attn_out.astype(jnp.bfloat16)  0.67 us
  transfers between devices with their start and end apart: 8, of which 6 were waited for; matrix products, arithmetic and copies ran while one was open for 0% of the time, Pallas kernels for 0%

profile of v3, /device:TPU:0, one launch (start us, length us, event | category | flops | bytes accessed | tf_op | source)
XLA Modules:
  0.0 30.3 jit_solution(12689884210731313384)
XLA Ops:
  0.6 0.0 copy-start.2
  0.6 0.0 copy-start.1
  0.7 0.0 copy-start
  0.7 4.7 %shard_map.121 = (f32[4,2560]{1,0:T(4,128)S(1)}, f32[4,2560]{1,0:T(4,128)S(1)}, f32[4,2560]{1,0:T(4,128)S(1)}, f32[4,2560]{1,0:T(4,128)S(1)}, bf16[16,16]{1,0:T(8,128)(2,1)S(1)}, /*index=5*/f32[4,1536]{1,0:T(4,128)S(1)}) custom-call(s32[1,16]{1,0:T(1,128)} %bitcast.6, s32[4]{0:T(128)} %refs_1_.1, s32[4]{0:T(128)} %refs_2_.1, bf16[16,2048]{1,0:T(8,128)(2,1)} %refs_3_.1, ...), custom_call_target="tpu_custom_call" | custom-call | flops 167772160 | bytes 10485760 | tf_op jit(solution)/shard_map/pallas_call | solution.py:120
  5.4 5.1 %collective-permute-start = (f32[4,2560]{1,0:T(4,128)S(1)}, f32[4,2560]{1,0:T(4,128)S(1)}, u32[]{:S(2)}, u32[]{:S(2)}) collective-permute-start(f32[4,2560]{1,0:T(4,128)S(1)} %get-tuple-element.16), channel_id=1, source_target_pairs={{0,12},{4,8},{8,4},{12,0},{1,13},{5,9},{9,5},{13,1},{2,14},{6,10},... | collective-permute-start | bytes 122888 | tf_op jit(solution)/shard_map/ppermute | solution.py:33
  10.5 0.0 collective-permute-start.1
  10.5 0.6 %collective-permute-start.2 = (f32[4,2560]{1,0:T(4,128)S(1)}, f32[4,2560]{1,0:T(4,128)S(1)}, u32[]{:S(2)}, u32[]{:S(2)}) collective-permute-start(f32[4,2560]{1,0:T(4,128)S(1)} %get-tuple-element.18), channel_id=1, source_target_pairs={{0,4},{4,0},{8,12},{12,8},{1,5},{5,1},{9,13},{13,9},{2,6},{6,2},{1... | collective-permute-start | bytes 122888 | tf_op jit(solution)/shard_map/ppermute | solution.py:33
  11.2 1.4 %collective-permute-done.refs_0_ = f32[4,2560]{1,0:T(4,128)S(1)} collective-permute-done((f32[4,2560]{1,0:T(4,128)S(1)}, f32[4,2560]{1,0:T(4,128)S(1)}, u32[]{:S(2)}, u32[]{:S(2)}) %collective-permute-start) | collective-permute-done | bytes 40992 | tf_op jit(solution)/shard_map/ppermute | solution.py:33
  12.5 2.9 %collective-permute-done.1.refs_1_ = f32[4,2560]{1,0:T(4,128)S(1)} collective-permute-done((f32[4,2560]{1,0:T(4,128)S(1)}, f32[4,2560]{1,0:T(4,128)S(1)}, u32[]{:S(2)}, u32[]{:S(2)}) %collective-permute-start.1) | collective-permute-done | bytes 40992 | tf_op jit(solution)/shard_map/ppermute | solution.py:33
  15.4 0.0 collective-permute-done.2.refs_2_
  15.4 0.0 copy-done.2
  15.4 0.0 copy-done.1
  15.4 0.8 %shard_map.122 = (bf16[4,2048]{1,0:T(4,128)(2,1)S(1)}, bf16[4,256]{1,0:T(4,128)(2,1)S(1)}, bf16[4,256]{1,0:T(4,128)(2,1)S(1)}) custom-call(f32[4,2560]{1,0:T(4,128)S(1)} %collective-permute-done.refs_0_, f32[4,2560]{1,0:T(4,128)S(1)} %collective-permute-done.1.refs_1_, f32[4,2560]{1,0:T(4,128)S(1)} %collective-permute-done.2.refs_2_, ...), custom_call_target="tpu_custom_call" | custom-call | flops 50331648 | bytes 3145728 | tf_op jit(solution)/shard_map/pallas_call | solution.py:218
  16.2 1.6 %collective-permute-start.5 = (bf16[4,2048]{1,0:T(4,128)(2,1)S(1)}, bf16[4,2048]{1,0:T(4,128)(2,1)S(1)}, u32[]{:S(2)}, u32[]{:S(2)}) collective-permute-start(bf16[4,2048]{1,0:T(4,128)(2,1)S(1)} %get-tuple-element.23.refs_0_), channel_id=1, source_target_pairs={{0,12},{4,8},{8,4},{12,0},{1,13},{5,9},{9,5},{13,1},{2,14},{6,10},... | collective-permute-start | bytes 49160 | tf_op jit(solution)/shard_map/ppermute | solution.py:33
  17.9 0.5 %collective-permute-start.4 = (bf16[4,2048]{1,0:T(4,128)(2,1)S(1)}, bf16[4,2048]{1,0:T(4,128)(2,1)S(1)}, u32[]{:S(2)}, u32[]{:S(2)}) collective-permute-start(bf16[4,2048]{1,0:T(4,128)(2,1)S(1)} %get-tuple-element.23.refs_0_), channel_id=1, source_target_pairs={{0,8},{4,12},{8,0},{12,4},{1,9},{5,13},{9,1},{13,5},{2,10},{6,14},... | collective-permute-start | bytes 49160 | tf_op jit(solution)/shard_map/ppermute | solution.py:33
  18.4 2.3 %collective-permute-start.3 = (bf16[4,2048]{1,0:T(4,128)(2,1)S(1)}, bf16[4,2048]{1,0:T(4,128)(2,1)S(1)}, u32[]{:S(2)}, u32[]{:S(2)}) collective-permute-start(bf16[4,2048]{1,0:T(4,128)(2,1)S(1)} %get-tuple-element.23.refs_0_), channel_id=1, source_target_pairs={{0,4},{4,0},{8,12},{12,8},{1,5},{5,1},{9,13},{13,9},{2,6},{6,2},{1... | collective-permute-start | bytes 49160 | tf_op jit(solution)/shard_map/ppermute | solution.py:33
  20.7 1.1 %collective-permute-done.5.refs_3_ = bf16[4,2048]{1,0:T(4,128)(2,1)S(1)} collective-permute-done((bf16[4,2048]{1,0:T(4,128)(2,1)S(1)}, bf16[4,2048]{1,0:T(4,128)(2,1)S(1)}, u32[]{:S(2)}, u32[]{:S(2)}) %collective-permute-start.5) | collective-permute-done | bytes 16416 | tf_op jit(solution)/shard_map/ppermute | solution.py:33
  21.8 0.7 %collective-permute-done.4.refs_2_ = bf16[4,2048]{1,0:T(4,128)(2,1)S(1)} collective-permute-done((bf16[4,2048]{1,0:T(4,128)(2,1)S(1)}, bf16[4,2048]{1,0:T(4,128)(2,1)S(1)}, u32[]{:S(2)}, u32[]{:S(2)}) %collective-permute-start.4) | collective-permute-done | bytes 16416 | tf_op jit(solution)/shard_map/ppermute | solution.py:33
  22.6 0.0 collective-permute-done.3.refs_1_
  22.6 0.0 copy-done
  22.6 1.4 %shard_map.123 = (bf16[16,2048]{1,0:T(8,128)(2,1)S(1)}, bf16[4,256]{1,0:T(4,128)(2,1)}, bf16[4,256]{1,0:T(4,128)(2,1)}) custom-call(bf16[16,16]{1,0:T(8,128)(2,1)S(1)} %get-tuple-element.15.picks_ref, bf16[4,256]{1,0:T(4,128)(2,1)S(1)} %get-tuple-element.21.keys_ref, bf16[4,256]{1,0:T(4,128)(2,1)S(1)} %get-tuple-element.22.values_ref, ...), custom_call_target="tpu_custom_call" | custom-call | flops 134217728 | bytes 8388608 | tf_op jit(solution)/shard_map/pallas_call | solution.py:265
  24.0 1.6 %collective-permute-start.6 = (bf16[16,2048]{1,0:T(8,128)(2,1)S(1)}, bf16[16,2048]{1,0:T(8,128)(2,1)S(1)}, u32[]{:S(2)}, u32[]{:S(2)}) collective-permute-start(bf16[16,2048]{1,0:T(8,128)(2,1)S(1)} %get-tuple-element.24), channel_id=1, source_target_pairs={{0,2},{1,3},{2,0},{3,1},{4,6},{5,7},{6,4},{7,5},{8,10},{9,11},{10,... | collective-permute-start | bytes 196616 | tf_op jit(solution)/shard_map/ppermute | solution.py:33
  25.5 2.8 %collective-permute-done.6 = bf16[16,2048]{1,0:T(8,128)(2,1)S(1)} collective-permute-done((bf16[16,2048]{1,0:T(8,128)(2,1)S(1)}, bf16[16,2048]{1,0:T(8,128)(2,1)S(1)}, u32[]{:S(2)}, u32[]{:S(2)}) %collective-permute-start.6) | collective-permute-done | bytes 65568 | tf_op jit(solution)/shard_map/ppermute | solution.py:33
  28.3 0.1 collective-permute-start.7
  28.4 1.2 %collective-permute-done.7 = bf16[16,2048]{1,0:T(8,128)(2,1)S(1)} collective-permute-done((bf16[16,2048]{1,0:T(8,128)(2,1)S(1)}, bf16[16,2048]{1,0:T(8,128)(2,1)S(1)}, u32[]{:S(2)}, u32[]{:S(2)}) %collective-permute-start.7) | collective-permute-done | bytes 65568 | tf_op jit(solution)/shard_map/ppermute | solution.py:33
  29.6 0.6 %add_convert_fusion = bf16[16,2048]{1,0:T(8,128)(2,1)} fusion(bf16[16,2048]{1,0:T(8,128)(2,1)S(1)} %collective-permute-done.7, bf16[16,2048]{1,0:T(8,128)(2,1)S(1)} %add_convert_fusion.1), kind=kLoop, calls=%fused_computation | loop fusion | flops 131072 | bytes 196608 | tf_op jit(solution)/shard_map/convert_element_type | solution.py:338
  (1 shorter events, 0.0 us)
Async XLA Ops:
  0.6 14.8 %copy-start.2 = (bf16[4,768,2,128]{3,2,1,0:T(2,128)(2,1)S(1)}, bf16[4,768,2,128]{3,2,1,0:T(2,128)(2,1)}, u32[]{:S(2)}) copy-start(bf16[4,768,2,128]{3,2,1,0:T(2,128)(2,1)} %param.16) | copy-start | bytes 4718596
  0.6 14.8 %copy-start.1 = (bf16[4,768,2,128]{3,2,1,0:T(2,128)(2,1)S(1)}, bf16[4,768,2,128]{3,2,1,0:T(2,128)(2,1)}, u32[]{:S(2)}) copy-start(bf16[4,768,2,128]{3,2,1,0:T(2,128)(2,1)} %param.15) | copy-start | bytes 4718596
  0.7 21.9 %copy-start = (bf16[2048,2048]{1,0:T(8,128)(2,1)S(1)}, bf16[2048,2048]{1,0:T(8,128)(2,1)}, u32[]{:S(2)}) copy-start(bf16[2048,2048]{1,0:T(8,128)(2,1)} %refs_4_.3) | copy-start | bytes 25165828
  5.4 7.1 %collective-permute-start = (f32[4,2560]{1,0:T(4,128)S(1)}, f32[4,2560]{1,0:T(4,128)S(1)}, u32[]{:S(2)}, u32[]{:S(2)}) collective-permute-start(f32[4,2560]{1,0:T(4,128)S(1)} %get-tuple-element.16), channel_id=1, source_target_pairs={{0,12},{4,8},{8,4},{12,0},{1,13},{5,9},{9,5},{13,1},{2,14},{6,10},... | collective-permute-start | bytes 122888 | tf_op jit(solution)/shard_map/ppermute | solution.py:33
  10.5 4.9 %collective-permute-start.1 = (f32[4,2560]{1,0:T(4,128)S(1)}, f32[4,2560]{1,0:T(4,128)S(1)}, u32[]{:S(2)}, u32[]{:S(2)}) collective-permute-start(f32[4,2560]{1,0:T(4,128)S(1)} %get-tuple-element.17), channel_id=1, source_target_pairs={{0,8},{4,12},{8,0},{12,4},{1,9},{5,13},{9,1},{13,5},{2,10},{6,14},... | collective-permute-start | bytes 122888 | tf_op jit(solution)/shard_map/ppermute | solution.py:33
  10.5 4.9 %collective-permute-start.2 = (f32[4,2560]{1,0:T(4,128)S(1)}, f32[4,2560]{1,0:T(4,128)S(1)}, u32[]{:S(2)}, u32[]{:S(2)}) collective-permute-start(f32[4,2560]{1,0:T(4,128)S(1)} %get-tuple-element.18), channel_id=1, source_target_pairs={{0,4},{4,0},{8,12},{12,8},{1,5},{5,1},{9,13},{13,9},{2,6},{6,2},{1... | collective-permute-start | bytes 122888 | tf_op jit(solution)/shard_map/ppermute | solution.py:33
  16.2 5.6 %collective-permute-start.5 = (bf16[4,2048]{1,0:T(4,128)(2,1)S(1)}, bf16[4,2048]{1,0:T(4,128)(2,1)S(1)}, u32[]{:S(2)}, u32[]{:S(2)}) collective-permute-start(bf16[4,2048]{1,0:T(4,128)(2,1)S(1)} %get-tuple-element.23.refs_0_), channel_id=1, source_target_pairs={{0,12},{4,8},{8,4},{12,0},{1,13},{5,9},{9,5},{13,1},{2,14},{6,10},... | collective-permute-start | bytes 49160 | tf_op jit(solution)/shard_map/ppermute | solution.py:33
  17.9 4.7 %collective-permute-start.4 = (bf16[4,2048]{1,0:T(4,128)(2,1)S(1)}, bf16[4,2048]{1,0:T(4,128)(2,1)S(1)}, u32[]{:S(2)}, u32[]{:S(2)}) collective-permute-start(bf16[4,2048]{1,0:T(4,128)(2,1)S(1)} %get-tuple-element.23.refs_0_), channel_id=1, source_target_pairs={{0,8},{4,12},{8,0},{12,4},{1,9},{5,13},{9,1},{13,5},{2,10},{6,14},... | collective-permute-start | bytes 49160 | tf_op jit(solution)/shard_map/ppermute | solution.py:33
  18.4 4.2 %collective-permute-start.3 = (bf16[4,2048]{1,0:T(4,128)(2,1)S(1)}, bf16[4,2048]{1,0:T(4,128)(2,1)S(1)}, u32[]{:S(2)}, u32[]{:S(2)}) collective-permute-start(bf16[4,2048]{1,0:T(4,128)(2,1)S(1)} %get-tuple-element.23.refs_0_), channel_id=1, source_target_pairs={{0,4},{4,0},{8,12},{12,8},{1,5},{5,1},{9,13},{13,9},{2,6},{6,2},{1... | collective-permute-start | bytes 49160 | tf_op jit(solution)/shard_map/ppermute | solution.py:33
  24.0 4.3 %collective-permute-start.6 = (bf16[16,2048]{1,0:T(8,128)(2,1)S(1)}, bf16[16,2048]{1,0:T(8,128)(2,1)S(1)}, u32[]{:S(2)}, u32[]{:S(2)}) collective-permute-start(bf16[16,2048]{1,0:T(8,128)(2,1)S(1)} %get-tuple-element.24), channel_id=1, source_target_pairs={{0,2},{1,3},{2,0},{3,1},{4,6},{5,7},{6,4},{7,5},{8,10},{9,11},{10,... | collective-permute-start | bytes 196616 | tf_op jit(solution)/shard_map/ppermute | solution.py:33
  28.3 1.3 %collective-permute-start.7 = (bf16[16,2048]{1,0:T(8,128)(2,1)S(1)}, bf16[16,2048]{1,0:T(8,128)(2,1)S(1)}, u32[]{:S(2)}, u32[]{:S(2)}) collective-permute-start(bf16[16,2048]{1,0:T(8,128)(2,1)S(1)} %add_convert_fusion.1), channel_id=1, source_target_pairs={{0,1},{1,0},{2,3},{3,2},{4,5},{5,4},{6,7},{7,6},{8,9},{9,8},{10,11... | collective-permute-start | bytes 196616 | tf_op jit(solution)/shard_map/ppermute | solution.py:33

commit v4 on v3

--- a/solution.py
+++ b/solution.py
@@ -37,6 +37,25 @@
     count = lax.axis_size(axis)
     came = [swap(blocks[d], axis, d) for d in range(count - 1, 0, -1)]
     return [blocks[0]] + came[::-1]
+
+
+def cross(block, distance):
+    wide, narrow = lax.axis_size("wide"), lax.axis_size("narrow")
+    return lax.ppermute(
+        block,
+        ("wide", "narrow"),
+        [
+            (w * narrow + n, (w ^ distance) * narrow + (n ^ 1))
+            for w in range(wide)
+            for n in range(narrow)
+        ],
+    )
+
+
+def cross_all(blocks):
+    own = cross(blocks[0], 0)
+    came = [cross(blocks[d], d) for d in range(len(blocks) - 1, 0, -1)]
+    return [own] + came[::-1]
 
 
 def tree_sum(terms):
@@ -152,13 +171,12 @@
 
 def attend_kernel(group, parts_count, kv_local, *refs):
     parts, refs = refs[:parts_count], refs[parts_count:]
-    keys, values, bias, heads_ref, keys_ref, values_ref, query_rows, mixed_rows = refs
+    keys, values, bias, heads_ref, latest_ref, query_rows, mixed_rows = refs
     slots, places, head_dim = keys.shape
     rows = kv_local * group
     query_cols, key_cols = rows * head_dim, kv_local * head_dim
     fresh = tree_sum([part[...] for part in parts]).astype(jnp.bfloat16)
-    keys_ref[...] = fresh[:, query_cols : query_cols + key_cols]
-    values_ref[...] = fresh[:, query_cols + key_cols :]
+    latest_ref[...] = fresh[:, query_cols:]
     fresh = fresh.astype(jnp.float32)
     for h in range(rows):
         query_rows[pl.ds(h, slots, stride=rows), :] = fresh[:, h * head_dim : (h + 1) * head_dim]
@@ -219,11 +237,10 @@
         functools.partial(attend_kernel, rows // kv_local, len(parts), kv_local),
         out_shape=[
             pltpu.VMEM((slots, query_cols), jnp.bfloat16),
-            pltpu.VMEM((slots, key_cols), jnp.bfloat16),
-            pltpu.VMEM((slots, key_cols), jnp.bfloat16),
+            pltpu.VMEM((slots, 2 * key_cols), jnp.bfloat16),
         ],
         in_specs=[in_vmem] * (len(parts) + 3),
-        out_specs=[in_vmem] * 3,
+        out_specs=[in_vmem] * 2,
         scratch_shapes=[
             pltpu.VMEM((slots * rows, head_dim), jnp.float32),
             pltpu.VMEM((slots * rows, head_dim), jnp.float32),
@@ -237,15 +254,8 @@
     )(*[kept_in_vmem(x) for x in parts], keys, values, kept_in_vmem(bias))
 
 
-def output_kernel(heads_count, picks_ref, keys_ref, values_ref, *refs):
-    heads, weight, refs = refs[:heads_count], refs[heads_count], refs[heads_count + 1 :]
-    out_ref, keys_hbm, values_hbm, sems = refs
-    copies = [
-        pltpu.make_async_copy(keys_ref, keys_hbm, sems.at[0]),
-        pltpu.make_async_copy(values_ref, values_hbm, sems.at[1]),
-    ]
-    for copy in copies:
-        copy.start()
+def output_kernel(heads_count, picks_ref, *refs):
+    heads, (weight, out_ref) = refs[:heads_count], refs[heads_count:]
     stacked = jnp.concatenate([h[...].astype(jnp.float32) for h in heads], axis=0)
     rows = lax.dot_general(
         picks_ref[...],
@@ -256,27 +266,20 @@
     out_ref[...] = jnp.dot(rows, weight[...], preferred_element_type=jnp.float32).astype(
         out_ref.dtype
     )
-    for copy in copies:
-        copy.wait()
-
-
-def project_out(picks, keys, values, heads, weight, dtype):
+
+
+def project_out(picks, heads, weight, dtype):
     requests = picks.shape[0]
     return pl.pallas_call(
         functools.partial(output_kernel, len(heads)),
-        out_shape=[
-            pltpu.VMEM((requests, weight.shape[1]), dtype),
-            pltpu.MemorySpace.HBM(keys.shape, keys.dtype),
-            pltpu.MemorySpace.HBM(values.shape, values.dtype),
-        ],
-        in_specs=[in_vmem] * (4 + len(heads)),
-        out_specs=[in_vmem, in_hbm, in_hbm],
-        scratch_shapes=[pltpu.SemaphoreType.DMA((2,))],
+        out_shape=pltpu.VMEM((requests, weight.shape[1]), dtype),
+        in_specs=[in_vmem] * (2 + len(heads)),
+        out_specs=in_vmem,
         compiler_params=pltpu.CompilerParams(vmem_limit_bytes=24 * mebibyte),
         cost_estimate=pl.CostEstimate(
             flops=2 * requests * weight.size, bytes_accessed=2 * weight.size, transcendentals=0
         ),
-    )(*[kept_in_vmem(x) for x in (picks, keys, values, *heads)], weight)
+    )(*[kept_in_vmem(x) for x in (picks, *heads)], weight)
 
 
 def per_device(
@@ -311,34 +314,34 @@
     keys = key_cache.reshape(slots, window * kv_local, head_dim)
     values = value_cache.reshape(slots, window * kv_local, head_dim)
     if direct_wide:
-        parts = exchange(parts, "wide")
+        values, bias = lax.optimization_barrier((values, bias))
+        keys, values = swap(keys, "narrow", 1), swap(values, "narrow", 1)
+    if direct_wide:
+        parts = cross_all(parts)
     else:
         parts = [lax.psum_scatter(parts[0], "wide", scatter_dimension=0, tiled=True)]
-    heads, keys_out, values_out = attend(parts[::-1], keys, values, bias, kv_local, w_query.shape[1])
+    heads, latest = attend(parts[::-1], keys, values, bias, kv_local, w_query.shape[1])
     if direct_wide:
-        heads = exchange([heads] * wide, "wide")
+        heads = cross_all([heads] * wide)
+        latest = swap(latest, "narrow", 1)
     else:
         heads = [lax.all_gather(heads, "wide", axis=0, tiled=True)]
     narrow = lax.axis_size("narrow")
     direct_narrow = is_direct(narrow)
-    sent, keys_out, values_out = project_out(
-        picks,
-        keys_out,
-        values_out,
-        heads,
-        w_out,
-        jnp.bfloat16 if direct_narrow else jnp.float32,
-    )
+    sent = project_out(picks, heads, w_out, jnp.bfloat16 if direct_narrow else jnp.float32)
     if direct_narrow:
+        attn_out = sent
         distance = narrow // 2
-        attn_out = sent
         while distance >= 1:
-            attn_out = attn_out.astype(jnp.float32) + swap(attn_out, "narrow", distance).astype(jnp.float32)
+            came = swap(attn_out, "narrow", distance | 1)
+            attn_out = (attn_out.astype(jnp.float32) + came.astype(jnp.float32)).astype(
+                jnp.bfloat16
+            )
             distance //= 2
-            attn_out = attn_out.astype(jnp.bfloat16)
     else:
         attn_out = lax.psum(sent, "narrow")
-    return (attn_out.astype(jnp.bfloat16), keys_out, values_out)
+    key_cols = w_key.shape[1]
+    return (attn_out.astype(jnp.bfloat16), latest[:, :key_cols], latest[:, key_cols:])
 
 
 def solution(mesh):

time: 30.4 us -> 30.3 us (level)
  waiting for transfers between devices: 10.2 us -> 9.06 us
  local copies, waits for them, and re-layouts: 0.01 us -> 0.59 us
  starting transfers between devices: 11.8 us -> 12.3 us
    ppermute x0 -> x8, starting transfers between devices: none -> 9.82 us  [cross(): lax.ppermute(block, ('wide', 'narrow'), [(w * narrow + n, (w ^ distance)...]
    ppermute x8 -> x5, starting transfers between devices: 11.8 us -> 2.45 us  [swap(): return lax.ppermute(block, axis, [(i, i ^ distance) for i in range(count)])]
    ppermute x8 -> x5, waiting for transfers between devices: 10.2 us -> 2.99 us  [swap(): return lax.ppermute(block, axis, [(i, i ^ distance) for i in range(count)])]
    ppermute x0 -> x8, waiting for transfers between devices: none -> 6.07 us  [cross(): lax.ppermute(block, ('wide', 'narrow'), [(w * narrow + n, (w ^ distance)...]
    slice x0 -> x1, local copies, waits for them, and re-layouts: none -> 0.59 us  [per_device(): latest[:, key_cols:]]
  transfers between devices with their start and end apart: 8 -> 13, of which waited for: 6 -> 6; matrix products, arithmetic and copies ran while one was open for 0% -> 2% of each run, Pallas kernels for 0% -> 0%
where the time goes in v4:
time: 30.3 us; the launch traced here: 30.2 us
  starting transfers between devices  12.3 us (41%)
  waiting for transfers between devices  9.06 us (30%)
  Pallas kernels  6.86 us (23%)
  between operations  0.71 us (2%)
  other arithmetic  0.67 us (2%)
  local copies, waits for them, and re-layouts  0.59 us (2%)
    ppermute x8, starting transfers between devices, cross(): lax.ppermute(block, ('wide', 'narrow'), [(w * narrow + n, (w ^ distance)...  9.82 us
    ppermute x8, waiting for transfers between devices, cross(): lax.ppermute(block, ('wide', 'narrow'), [(w * narrow + n, (w ^ distance)...  6.07 us
    pallas_call x1, Pallas kernels, project(): pl.pallas_call(functools.partial(project_kernel, slots, direct, pieces, c...  4.73 us
    ppermute x5, waiting for transfers between devices, swap(): return lax.ppermute(block, axis, [(i, i ^ distance) for i in range(count)])  2.99 us
    ppermute x5, starting transfers between devices, swap(): return lax.ppermute(block, axis, [(i, i ^ distance) for i in range(count)])  2.45 us
    pallas_call x1, Pallas kernels, project_out(): pl.pallas_call(functools.partial(output_kernel, len(heads)), out_shape=pl...  1.34 us
    pallas_call x1, Pallas kernels, attend(): pl.pallas_call(functools.partial(attend_kernel, rows // kv_local, len(par...  0.79 us
    convert_element_type x2, other arithmetic, per_device(): (attn_out.astype(jnp.float32) + came.astype(jnp.float32)).astype(jnp.bflo...  0.67 us
  transfers between devices with their start and end apart: 13, of which 6 were waited for; matrix products, arithmetic and copies ran while one was open for 2% of the time, Pallas kernels for 0%

profile of v4, /device:TPU:0, one launch (start us, length us, event | category | flops | bytes accessed | tf_op | source)
XLA Modules:
  0.0 30.2 jit_solution(4492295481993145120)
XLA Ops:
  0.6 0.0 copy-start.1
  0.7 4.7 %shard_map.121 = (f32[4,2560]{1,0:T(4,128)S(1)}, f32[4,2560]{1,0:T(4,128)S(1)}, f32[4,2560]{1,0:T(4,128)S(1)}, f32[4,2560]{1,0:T(4,128)S(1)}, bf16[16,16]{1,0:T(8,128)(2,1)S(1)}, /*index=5*/f32[4,1536]{1,0:T(4,128)S(1)}) custom-call(s32[1,16]{1,0:T(1,128)} %bitcast.4, s32[4]{0:T(128)} %refs_1_.1, s32[4]{0:T(128)} %refs_2_.1, bf16[16,2048]{1,0:T(8,128)(2,1)} %refs_3_.1, ...), custom_call_target="tpu_custom_call" | custom-call | flops 167772160 | bytes 10485760 | tf_op jit(solution)/shard_map/pallas_call | solution.py:139
  5.4 0.5 %collective-permute-start.5 = (bf16[4,1536,128]{2,1,0:T(8,128)(2,1)S(1)}, bf16[4,1536,128]{2,1,0:T(8,128)(2,1)S(1)}, u32[]{:S(2)}, u32[]{:S(2)}) collective-permute-start(bf16[4,1536,128]{2,1,0:T(8,128)(2,1)S(1)} %bitcast.5), channel_id=1, source_target_pairs={{0,1},{1,0},{2,3},{3,2},{4,5},{5,4},{6,7},{7,6},{8,9},{9,8},{10,11... | collective-permute-start | bytes 4718600 | tf_op jit(solution)/shard_map/ppermute | solution.py:33
  5.9 0.1 collective-permute-start.4
  6.0 4.7 %collective-permute-start = (f32[4,2560]{1,0:T(4,128)S(1)}, f32[4,2560]{1,0:T(4,128)S(1)}, u32[]{:S(2)}, u32[]{:S(2)}) collective-permute-start(f32[4,2560]{1,0:T(4,128)S(1)} %get-tuple-element.14), channel_id=1, source_target_pairs={{0,13},{1,12},{2,15},{3,14},{4,9},{5,8},{6,11},{7,10},{8,5},{9,4},... | collective-permute-start | bytes 122888 | tf_op jit(solution)/shard_map/ppermute | solution.py:44
  10.7 0.0 collective-permute-start.1
  10.7 0.6 %collective-permute-start.2 = (f32[4,2560]{1,0:T(4,128)S(1)}, f32[4,2560]{1,0:T(4,128)S(1)}, u32[]{:S(2)}, u32[]{:S(2)}) collective-permute-start(f32[4,2560]{1,0:T(4,128)S(1)} %get-tuple-element.16), channel_id=1, source_target_pairs={{0,5},{1,4},{2,7},{3,6},{4,1},{5,0},{6,3},{7,2},{8,13},{9,12},{10,... | collective-permute-start | bytes 122888 | tf_op jit(solution)/shard_map/ppermute | solution.py:44
  11.3 1.3 %collective-permute-done.refs_0_ = f32[4,2560]{1,0:T(4,128)S(1)} collective-permute-done((f32[4,2560]{1,0:T(4,128)S(1)}, f32[4,2560]{1,0:T(4,128)S(1)}, u32[]{:S(2)}, u32[]{:S(2)}) %collective-permute-start) | collective-permute-done | bytes 40992 | tf_op jit(solution)/shard_map/ppermute | solution.py:44
  12.7 0.2 collective-permute-start.3
  12.9 2.3 %collective-permute-done.1.refs_1_ = f32[4,2560]{1,0:T(4,128)S(1)} collective-permute-done((f32[4,2560]{1,0:T(4,128)S(1)}, f32[4,2560]{1,0:T(4,128)S(1)}, u32[]{:S(2)}, u32[]{:S(2)}) %collective-permute-start.1) | collective-permute-done | bytes 40992 | tf_op jit(solution)/shard_map/ppermute | solution.py:44
  15.2 0.0 collective-permute-done.2.refs_2_
  15.2 0.0 collective-permute-done.3.refs_3_
  15.2 0.0 collective-permute-done.5.refs_5_
  15.2 0.0 collective-permute-done.4.refs_4_
  15.2 0.8 %shard_map.122 = (bf16[4,2048]{1,0:T(4,128)(2,1)S(1)}, bf16[4,512]{1,0:T(4,128)(2,1)S(1)}) custom-call(f32[4,2560]{1,0:T(4,128)S(1)} %collective-permute-done.refs_0_, f32[4,2560]{1,0:T(4,128)S(1)} %collective-permute-done.1.refs_1_, f32[4,2560]{1,0:T(4,128)S(1)} %collective-permute-done.2.refs_2_, f32[4,2560]{1,0:T(4,128)S(1)} %collective-permute-done.3.refs_3_, ...), custom_call_target="tpu_custom_call" | custom-call | flops 50331648 | bytes 3145728 | tf_op jit(solution)/shard_map/pallas_call | solution.py:236
  16.0 2.4 %collective-permute-start.9 = (bf16[4,2048]{1,0:T(4,128)(2,1)S(1)}, bf16[4,2048]{1,0:T(4,128)(2,1)S(1)}, u32[]{:S(2)}, u32[]{:S(2)}) collective-permute-start(bf16[4,2048]{1,0:T(4,128)(2,1)S(1)} %get-tuple-element.21), channel_id=1, source_target_pairs={{0,13},{1,12},{2,15},{3,14},{4,9},{5,8},{6,11},{7,10},{8,5},{9,4},... | collective-permute-start | bytes 49160 | tf_op jit(solution)/shard_map/ppermute | solution.py:44
  18.5 0.0 collective-permute-start.8
  18.5 1.6 %collective-permute-start.7 = (bf16[4,2048]{1,0:T(4,128)(2,1)S(1)}, bf16[4,2048]{1,0:T(4,128)(2,1)S(1)}, u32[]{:S(2)}, u32[]{:S(2)}) collective-permute-start(bf16[4,2048]{1,0:T(4,128)(2,1)S(1)} %get-tuple-element.21), channel_id=1, source_target_pairs={{0,5},{1,4},{2,7},{3,6},{4,1},{5,0},{6,3},{7,2},{8,13},{9,12},{10,... | collective-permute-start | bytes 49160 | tf_op jit(solution)/shard_map/ppermute | solution.py:44
  20.1 0.2 collective-permute-start.6
  20.3 0.7 %collective-permute-done.9.refs_3_ = bf16[4,2048]{1,0:T(4,128)(2,1)S(1)} collective-permute-done((bf16[4,2048]{1,0:T(4,128)(2,1)S(1)}, bf16[4,2048]{1,0:T(4,128)(2,1)S(1)}, u32[]{:S(2)}, u32[]{:S(2)}) %collective-permute-start.9) | collective-permute-done | bytes 16416 | tf_op jit(solution)/shard_map/ppermute | solution.py:44
  21.0 1.7 %collective-permute-done.8.refs_2_ = bf16[4,2048]{1,0:T(4,128)(2,1)S(1)} collective-permute-done((bf16[4,2048]{1,0:T(4,128)(2,1)S(1)}, bf16[4,2048]{1,0:T(4,128)(2,1)S(1)}, u32[]{:S(2)}, u32[]{:S(2)}) %collective-permute-start.8) | collective-permute-done | bytes 16416 | tf_op jit(solution)/shard_map/ppermute | solution.py:44
  22.7 0.0 collective-permute-done.7.refs_1_
  22.7 0.0 collective-permute-done.6.refs_0_
  22.7 1.3 %shard_map.123 = bf16[16,2048]{1,0:T(8,128)(2,1)S(1)} custom-call(bf16[16,16]{1,0:T(8,128)(2,1)S(1)} %get-tuple-element.13.picks_ref, bf16[4,2048]{1,0:T(4,128)(2,1)S(1)} %collective-permute-done.6.refs_0_, bf16[4,2048]{1,0:T(4,128)(2,1)S(1)} %collective-permute-done.7.refs_1_, bf16[4,2048]{1,0:T(4,128)(2,1)S(1)} %collective-permute-done.8.refs_2_, ...), custom_call_target="tpu_custom_call" | custom-call | flops 134217728 | bytes 8388608 | tf_op jit(solution)/shard_map/pallas_call | solution.py:273
  24.1 1.3 %collective-permute-start.10 = (bf16[16,2048]{1,0:T(8,128)(2,1)S(1)}, bf16[16,2048]{1,0:T(8,128)(2,1)S(1)}, u32[]{:S(2)}, u32[]{:S(2)}) collective-permute-start(bf16[16,2048]{1,0:T(8,128)(2,1)S(1)} %shard_map.123), channel_id=1, source_target_pairs={{0,3},{1,2},{2,1},{3,0},{4,7},{5,6},{6,5},{7,4},{8,11},{9,10},{10,... | collective-permute-start | bytes 196616 | tf_op jit(solution)/shard_map/ppermute | solution.py:33
  25.3 0.4 %collective-permute-start.12 = (bf16[4,512]{1,0:T(4,128)(2,1)S(1)}, bf16[4,512]{1,0:T(4,128)(2,1)S(1)}, u32[]{:S(2)}, u32[]{:S(2)}) collective-permute-start(bf16[4,512]{1,0:T(4,128)(2,1)S(1)} %get-tuple-element.22), channel_id=1, source_target_pairs={{0,1},{1,0},{2,3},{3,2},{4,5},{5,4},{6,7},{7,6},{8,9},{9,8},{10,11... | collective-permute-start | bytes 12296 | tf_op jit(solution)/shard_map/ppermute | solution.py:33
  25.7 2.4 %collective-permute-done.10 = bf16[16,2048]{1,0:T(8,128)(2,1)S(1)} collective-permute-done((bf16[16,2048]{1,0:T(8,128)(2,1)S(1)}, bf16[16,2048]{1,0:T(8,128)(2,1)S(1)}, u32[]{:S(2)}, u32[]{:S(2)}) %collective-permute-start.10) | collective-permute-done | bytes 65568 | tf_op jit(solution)/shard_map/ppermute | solution.py:33
  28.2 0.2 collective-permute-start.11
  28.4 0.0 collective-permute-done.12
  28.4 0.6 %fusion = (bf16[4,256]{1,0:T(4,128)(2,1)}, bf16[4,256]{1,0:T(4,128)(2,1)}) fusion(bf16[4,512]{1,0:T(4,128)(2,1)S(1)} %collective-permute-done.12), kind=kLoop, calls=%fused_computation.2 | loop fusion | bytes 8192 | tf_op jit(solution)/shard_map/slice | solution.py:344
  29.0 0.5 %collective-permute-done.11 = bf16[16,2048]{1,0:T(8,128)(2,1)S(1)} collective-permute-done((bf16[16,2048]{1,0:T(8,128)(2,1)S(1)}, bf16[16,2048]{1,0:T(8,128)(2,1)S(1)}, u32[]{:S(2)}, u32[]{:S(2)}) %collective-permute-start.11) | collective-permute-done | bytes 65568 | tf_op jit(solution)/shard_map/ppermute | solution.py:33
  29.5 0.6 %add_convert_fusion = bf16[16,2048]{1,0:T(8,128)(2,1)} fusion(bf16[16,2048]{1,0:T(8,128)(2,1)S(1)} %collective-permute-done.11, bf16[16,2048]{1,0:T(8,128)(2,1)S(1)} %add_convert_fusion.1), kind=kLoop, calls=%fused_computation | loop fusion | flops 131072 | bytes 196608 | tf_op jit(solution)/shard_map/convert_element_type | solution.py:337
  (4 shorter events, 0.0 us)
Async XLA Ops:
  0.6 4.8 %copy-start.1 = (bf16[4,768,2,128]{3,2,1,0:T(2,128)(2,1)S(1)}, bf16[4,768,2,128]{3,2,1,0:T(2,128)(2,1)}, u32[]{:S(2)}) copy-start(bf16[4,768,2,128]{3,2,1,0:T(2,128)(2,1)} %param.16) | copy-start | bytes 4718596
  0.6 22.1 %copy-start = (bf16[2048,2048]{1,0:T(8,128)(2,1)S(1)}, bf16[2048,2048]{1,0:T(8,128)(2,1)}, u32[]{:S(2)}) copy-start(bf16[2048,2048]{1,0:T(8,128)(2,1)} %refs_4_.3) | copy-start | bytes 25165828
  5.4 9.8 %collective-permute-start.5 = (bf16[4,1536,128]{2,1,0:T(8,128)(2,1)S(1)}, bf16[4,1536,128]{2,1,0:T(8,128)(2,1)S(1)}, u32[]{:S(2)}, u32[]{:S(2)}) collective-permute-start(bf16[4,1536,128]{2,1,0:T(8,128)(2,1)S(1)} %bitcast.5), channel_id=1, source_target_pairs={{0,1},{1,0},{2,3},{3,2},{4,5},{5,4},{6,7},{7,6},{8,9},{9,8},{10,11... | collective-permute-start | bytes 4718600 | tf_op jit(solution)/shard_map/ppermute | solution.py:33
  5.9 9.3 %collective-permute-start.4 = (bf16[4,1536,128]{2,1,0:T(8,128)(2,1)}, bf16[4,1536,128]{2,1,0:T(8,128)(2,1)S(1)}, u32[]{:S(2)}, u32[]{:S(2)}) collective-permute-start(bf16[4,1536,128]{2,1,0:T(8,128)(2,1)} %bitcast.6), channel_id=1, source_target_pairs={{0,1},{1,0},{2,3},{3,2},{4,5},{5,4},{6,7},{7,6},{8,9},{9,8},{10,11... | collective-permute-start | bytes 4718600 | tf_op jit(solution)/shard_map/ppermute | solution.py:33
  6.0 6.7 %collective-permute-start = (f32[4,2560]{1,0:T(4,128)S(1)}, f32[4,2560]{1,0:T(4,128)S(1)}, u32[]{:S(2)}, u32[]{:S(2)}) collective-permute-start(f32[4,2560]{1,0:T(4,128)S(1)} %get-tuple-element.14), channel_id=1, source_target_pairs={{0,13},{1,12},{2,15},{3,14},{4,9},{5,8},{6,11},{7,10},{8,5},{9,4},... | collective-permute-start | bytes 122888 | tf_op jit(solution)/shard_map/ppermute | solution.py:44
  10.7 4.5 %collective-permute-start.1 = (f32[4,2560]{1,0:T(4,128)S(1)}, f32[4,2560]{1,0:T(4,128)S(1)}, u32[]{:S(2)}, u32[]{:S(2)}) collective-permute-start(f32[4,2560]{1,0:T(4,128)S(1)} %get-tuple-element.15), channel_id=1, source_target_pairs={{0,9},{1,8},{2,11},{3,10},{4,13},{5,12},{6,15},{7,14},{8,1},{9,0},... | collective-permute-start | bytes 122888 | tf_op jit(solution)/shard_map/ppermute | solution.py:44
  10.7 4.5 %collective-permute-start.2 = (f32[4,2560]{1,0:T(4,128)S(1)}, f32[4,2560]{1,0:T(4,128)S(1)}, u32[]{:S(2)}, u32[]{:S(2)}) collective-permute-start(f32[4,2560]{1,0:T(4,128)S(1)} %get-tuple-element.16), channel_id=1, source_target_pairs={{0,5},{1,4},{2,7},{3,6},{4,1},{5,0},{6,3},{7,2},{8,13},{9,12},{10,... | collective-permute-start | bytes 122888 | tf_op jit(solution)/shard_map/ppermute | solution.py:44
  12.7 2.5 %collective-permute-start.3 = (f32[4,2560]{1,0:T(4,128)S(1)}, f32[4,2560]{1,0:T(4,128)S(1)}, u32[]{:S(2)}, u32[]{:S(2)}) collective-permute-start(f32[4,2560]{1,0:T(4,128)S(1)} %get-tuple-element.17), channel_id=1, source_target_pairs={{0,1},{1,0},{2,3},{3,2},{4,5},{5,4},{6,7},{7,6},{8,9},{9,8},{10,11... | collective-permute-start | bytes 122888 | tf_op jit(solution)/shard_map/ppermute | solution.py:44
  16.0 5.0 %collective-permute-start.9 = (bf16[4,2048]{1,0:T(4,128)(2,1)S(1)}, bf16[4,2048]{1,0:T(4,128)(2,1)S(1)}, u32[]{:S(2)}, u32[]{:S(2)}) collective-permute-start(bf16[4,2048]{1,0:T(4,128)(2,1)S(1)} %get-tuple-element.21), channel_id=1, source_target_pairs={{0,13},{1,12},{2,15},{3,14},{4,9},{5,8},{6,11},{7,10},{8,5},{9,4},... | collective-permute-start | bytes 49160 | tf_op jit(solution)/shard_map/ppermute | solution.py:44
  18.5 4.2 %collective-permute-start.8 = (bf16[4,2048]{1,0:T(4,128)(2,1)S(1)}, bf16[4,2048]{1,0:T(4,128)(2,1)S(1)}, u32[]{:S(2)}, u32[]{:S(2)}) collective-permute-start(bf16[4,2048]{1,0:T(4,128)(2,1)S(1)} %get-tuple-element.21), channel_id=1, source_target_pairs={{0,9},{1,8},{2,11},{3,10},{4,13},{5,12},{6,15},{7,14},{8,1},{9,0},... | collective-permute-start | bytes 49160 | tf_op jit(solution)/shard_map/ppermute | solution.py:44
  18.5 4.2 %collective-permute-start.7 = (bf16[4,2048]{1,0:T(4,128)(2,1)S(1)}, bf16[4,2048]{1,0:T(4,128)(2,1)S(1)}, u32[]{:S(2)}, u32[]{:S(2)}) collective-permute-start(bf16[4,2048]{1,0:T(4,128)(2,1)S(1)} %get-tuple-element.21), channel_id=1, source_target_pairs={{0,5},{1,4},{2,7},{3,6},{4,1},{5,0},{6,3},{7,2},{8,13},{9,12},{10,... | collective-permute-start | bytes 49160 | tf_op jit(solution)/shard_map/ppermute | solution.py:44
  20.1 2.6 %collective-permute-start.6 = (bf16[4,2048]{1,0:T(4,128)(2,1)S(1)}, bf16[4,2048]{1,0:T(4,128)(2,1)S(1)}, u32[]{:S(2)}, u32[]{:S(2)}) collective-permute-start(bf16[4,2048]{1,0:T(4,128)(2,1)S(1)} %get-tuple-element.21), channel_id=1, source_target_pairs={{0,1},{1,0},{2,3},{3,2},{4,5},{5,4},{6,7},{7,6},{8,9},{9,8},{10,11... | collective-permute-start | bytes 49160 | tf_op jit(solution)/shard_map/ppermute | solution.py:44
  24.1 4.1 %collective-permute-start.10 = (bf16[16,2048]{1,0:T(8,128)(2,1)S(1)}, bf16[16,2048]{1,0:T(8,128)(2,1)S(1)}, u32[]{:S(2)}, u32[]{:S(2)}) collective-permute-start(bf16[16,2048]{1,0:T(8,128)(2,1)S(1)} %shard_map.123), channel_id=1, source_target_pairs={{0,3},{1,2},{2,1},{3,0},{4,7},{5,6},{6,5},{7,4},{8,11},{9,10},{10,... | collective-permute-start | bytes 196616 | tf_op jit(solution)/shard_map/ppermute | solution.py:33
  25.3 3.0 %collective-permute-start.12 = (bf16[4,512]{1,0:T(4,128)(2,1)S(1)}, bf16[4,512]{1,0:T(4,128)(2,1)S(1)}, u32[]{:S(2)}, u32[]{:S(2)}) collective-permute-start(bf16[4,512]{1,0:T(4,128)(2,1)S(1)} %get-tuple-element.22), channel_id=1, source_target_pairs={{0,1},{1,0},{2,3},{3,2},{4,5},{5,4},{6,7},{7,6},{8,9},{9,8},{10,11... | collective-permute-start | bytes 12296 | tf_op jit(solution)/shard_map/ppermute | solution.py:33
  28.2 1.3 %collective-permute-start.11 = (bf16[16,2048]{1,0:T(8,128)(2,1)S(1)}, bf16[16,2048]{1,0:T(8,128)(2,1)S(1)}, u32[]{:S(2)}, u32[]{:S(2)}) collective-permute-start(bf16[16,2048]{1,0:T(8,128)(2,1)S(1)} %add_convert_fusion.1), channel_id=1, source_target_pairs={{0,1},{1,0},{2,3},{3,2},{4,5},{5,4},{6,7},{7,6},{8,9},{9,8},{10,11... | collective-permute-start | bytes 196616 | tf_op jit(solution)/shard_map/ppermute | solution.py:33

commit v5 on v3

--- a/solution.py
+++ b/solution.py
@@ -198,13 +198,17 @@
     own = [jnp.exp((latest[s] - top[s]) * scale) for s in every]
     total = [jnp.sum(spread[s], axis=1, keepdims=True) + own[s] for s in every]
     mixed = [
-        jnp.dot(spread[s].astype(jnp.bfloat16), values[s], preferred_element_type=jnp.float32)
+        jnp.dot(
+            (spread[s] / total[s]).astype(jnp.bfloat16),
+            values[s],
+            preferred_element_type=jnp.float32,
+        )
         for s in every
     ]
     for s in every:
         mixed_rows[s * rows : (s + 1) * rows, :] = (
-            mixed[s] + own[s] * spread_new(s, query_cols + key_cols)
-        ) / total[s]
+            mixed[s] + own[s] / total[s] * spread_new(s, query_cols + key_cols)
+        )
     for h in range(rows):
         heads_ref[:, h * head_dim : (h + 1) * head_dim] = mixed_rows[
             pl.ds(h, slots, stride=rows), :

time: 30.4 us -> 30.5 us (level)
  no operation moved by 1% of the time
where the time goes in v5:
time: 30.5 us; the launch traced here: 30.4 us
  starting transfers between devices  11.8 us (39%)
  waiting for transfers between devices  10.2 us (33%)
  Pallas kernels  6.98 us (23%)
  between operations  0.71 us (2%)
  other arithmetic  0.67 us (2%)
    ppermute x8, starting transfers between devices, swap(): return lax.ppermute(block, axis, [(i, i ^ distance) for i in range(count)])  11.8 us
    ppermute x8, waiting for transfers between devices, swap(): return lax.ppermute(block, axis, [(i, i ^ distance) for i in range(count)])  10.2 us
    pallas_call x1, Pallas kernels, project(): pl.pallas_call(functools.partial(project_kernel, slots, direct, pieces, c...  4.73 us
    pallas_call x1, Pallas kernels, project_out(): pl.pallas_call(functools.partial(output_kernel, len(heads)), out_shape=[p...  1.37 us
    pallas_call x1, Pallas kernels, attend(): pl.pallas_call(functools.partial(attend_kernel, rows // kv_local, len(par...  0.88 us
    convert_element_type x2, other arithmetic, per_device(): attn_out = attn_out.astype(jnp.bfloat16)  0.67 us
  transfers between devices with their start and end apart: 8, of which 6 were waited for; matrix products, arithmetic and copies ran while one was open for 0% of the time, Pallas kernels for 0%

profile of v5, /device:TPU:0, one launch (start us, length us, event | category | flops | bytes accessed | tf_op | source)
XLA Modules:
  0.0 30.4 jit_solution(5595512706755204264)
XLA Ops:
  0.6 0.0 copy-start.2
  0.6 0.0 copy-start.1
  0.7 0.0 copy-start
  0.7 4.7 %shard_map.121 = (f32[4,2560]{1,0:T(4,128)S(1)}, f32[4,2560]{1,0:T(4,128)S(1)}, f32[4,2560]{1,0:T(4,128)S(1)}, f32[4,2560]{1,0:T(4,128)S(1)}, bf16[16,16]{1,0:T(8,128)(2,1)S(1)}, /*index=5*/f32[4,1536]{1,0:T(4,128)S(1)}) custom-call(s32[1,16]{1,0:T(1,128)} %bitcast.6, s32[4]{0:T(128)} %refs_1_.1, s32[4]{0:T(128)} %refs_2_.1, bf16[16,2048]{1,0:T(8,128)(2,1)} %refs_3_.1, ...), custom_call_target="tpu_custom_call" | custom-call | flops 167772160 | bytes 10485760 | tf_op jit(solution)/shard_map/pallas_call | solution.py:120
  5.4 5.1 %collective-permute-start = (f32[4,2560]{1,0:T(4,128)S(1)}, f32[4,2560]{1,0:T(4,128)S(1)}, u32[]{:S(2)}, u32[]{:S(2)}) collective-permute-start(f32[4,2560]{1,0:T(4,128)S(1)} %get-tuple-element.16), channel_id=1, source_target_pairs={{0,12},{4,8},{8,4},{12,0},{1,13},{5,9},{9,5},{13,1},{2,14},{6,10},... | collective-permute-start | bytes 122888 | tf_op jit(solution)/shard_map/ppermute | solution.py:33
  10.5 0.0 collective-permute-start.1
  10.5 0.6 %collective-permute-start.2 = (f32[4,2560]{1,0:T(4,128)S(1)}, f32[4,2560]{1,0:T(4,128)S(1)}, u32[]{:S(2)}, u32[]{:S(2)}) collective-permute-start(f32[4,2560]{1,0:T(4,128)S(1)} %get-tuple-element.18), channel_id=1, source_target_pairs={{0,4},{4,0},{8,12},{12,8},{1,5},{5,1},{9,13},{13,9},{2,6},{6,2},{1... | collective-permute-start | bytes 122888 | tf_op jit(solution)/shard_map/ppermute | solution.py:33
  11.2 1.4 %collective-permute-done.refs_0_ = f32[4,2560]{1,0:T(4,128)S(1)} collective-permute-done((f32[4,2560]{1,0:T(4,128)S(1)}, f32[4,2560]{1,0:T(4,128)S(1)}, u32[]{:S(2)}, u32[]{:S(2)}) %collective-permute-start) | collective-permute-done | bytes 40992 | tf_op jit(solution)/shard_map/ppermute | solution.py:33
  12.5 2.9 %collective-permute-done.1.refs_1_ = f32[4,2560]{1,0:T(4,128)S(1)} collective-permute-done((f32[4,2560]{1,0:T(4,128)S(1)}, f32[4,2560]{1,0:T(4,128)S(1)}, u32[]{:S(2)}, u32[]{:S(2)}) %collective-permute-start.1) | collective-permute-done | bytes 40992 | tf_op jit(solution)/shard_map/ppermute | solution.py:33
  15.4 0.0 collective-permute-done.2.refs_2_
  15.4 0.0 copy-done.2
  15.4 0.0 copy-done.1
  15.4 0.9 %shard_map.122 = (bf16[4,2048]{1,0:T(4,128)(2,1)S(1)}, bf16[4,256]{1,0:T(4,128)(2,1)S(1)}, bf16[4,256]{1,0:T(4,128)(2,1)S(1)}) custom-call(f32[4,2560]{1,0:T(4,128)S(1)} %collective-permute-done.refs_0_, f32[4,2560]{1,0:T(4,128)S(1)} %collective-permute-done.1.refs_1_, f32[4,2560]{1,0:T(4,128)S(1)} %collective-permute-done.2.refs_2_, ...), custom_call_target="tpu_custom_call" | custom-call | flops 50331648 | bytes 3145728 | tf_op jit(solution)/shard_map/pallas_call | solution.py:222
  16.3 1.6 %collective-permute-start.5 = (bf16[4,2048]{1,0:T(4,128)(2,1)S(1)}, bf16[4,2048]{1,0:T(4,128)(2,1)S(1)}, u32[]{:S(2)}, u32[]{:S(2)}) collective-permute-start(bf16[4,2048]{1,0:T(4,128)(2,1)S(1)} %get-tuple-element.23.refs_0_), channel_id=1, source_target_pairs={{0,12},{4,8},{8,4},{12,0},{1,13},{5,9},{9,5},{13,1},{2,14},{6,10},... | collective-permute-start | bytes 49160 | tf_op jit(solution)/shard_map/ppermute | solution.py:33
  18.0 0.5 %collective-permute-start.4 = (bf16[4,2048]{1,0:T(4,128)(2,1)S(1)}, bf16[4,2048]{1,0:T(4,128)(2,1)S(1)}, u32[]{:S(2)}, u32[]{:S(2)}) collective-permute-start(bf16[4,2048]{1,0:T(4,128)(2,1)S(1)} %get-tuple-element.23.refs_0_), channel_id=1, source_target_pairs={{0,8},{4,12},{8,0},{12,4},{1,9},{5,13},{9,1},{13,5},{2,10},{6,14},... | collective-permute-start | bytes 49160 | tf_op jit(solution)/shard_map/ppermute | solution.py:33
  18.5 2.3 %collective-permute-start.3 = (bf16[4,2048]{1,0:T(4,128)(2,1)S(1)}, bf16[4,2048]{1,0:T(4,128)(2,1)S(1)}, u32[]{:S(2)}, u32[]{:S(2)}) collective-permute-start(bf16[4,2048]{1,0:T(4,128)(2,1)S(1)} %get-tuple-element.23.refs_0_), channel_id=1, source_target_pairs={{0,4},{4,0},{8,12},{12,8},{1,5},{5,1},{9,13},{13,9},{2,6},{6,2},{1... | collective-permute-start | bytes 49160 | tf_op jit(solution)/shard_map/ppermute | solution.py:33
  20.8 1.1 %collective-permute-done.5.refs_3_ = bf16[4,2048]{1,0:T(4,128)(2,1)S(1)} collective-permute-done((bf16[4,2048]{1,0:T(4,128)(2,1)S(1)}, bf16[4,2048]{1,0:T(4,128)(2,1)S(1)}, u32[]{:S(2)}, u32[]{:S(2)}) %collective-permute-start.5) | collective-permute-done | bytes 16416 | tf_op jit(solution)/shard_map/ppermute | solution.py:33
  21.9 0.7 %collective-permute-done.4.refs_2_ = bf16[4,2048]{1,0:T(4,128)(2,1)S(1)} collective-permute-done((bf16[4,2048]{1,0:T(4,128)(2,1)S(1)}, bf16[4,2048]{1,0:T(4,128)(2,1)S(1)}, u32[]{:S(2)}, u32[]{:S(2)}) %collective-permute-start.4) | collective-permute-done | bytes 16416 | tf_op jit(solution)/shard_map/ppermute | solution.py:33
  22.7 0.0 collective-permute-done.3.refs_1_
  22.7 0.0 copy-done
  22.7 1.4 %shard_map.123 = (bf16[16,2048]{1,0:T(8,128)(2,1)S(1)}, bf16[4,256]{1,0:T(4,128)(2,1)}, bf16[4,256]{1,0:T(4,128)(2,1)}) custom-call(bf16[16,16]{1,0:T(8,128)(2,1)S(1)} %get-tuple-element.15.picks_ref, bf16[4,256]{1,0:T(4,128)(2,1)S(1)} %get-tuple-element.21.keys_ref, bf16[4,256]{1,0:T(4,128)(2,1)S(1)} %get-tuple-element.22.values_ref, ...), custom_call_target="tpu_custom_call" | custom-call | flops 134217728 | bytes 8388608 | tf_op jit(solution)/shard_map/pallas_call | solution.py:269
  24.1 1.6 %collective-permute-start.6 = (bf16[16,2048]{1,0:T(8,128)(2,1)S(1)}, bf16[16,2048]{1,0:T(8,128)(2,1)S(1)}, u32[]{:S(2)}, u32[]{:S(2)}) collective-permute-start(bf16[16,2048]{1,0:T(8,128)(2,1)S(1)} %get-tuple-element.24), channel_id=1, source_target_pairs={{0,2},{1,3},{2,0},{3,1},{4,6},{5,7},{6,4},{7,5},{8,10},{9,11},{10,... | collective-permute-start | bytes 196616 | tf_op jit(solution)/shard_map/ppermute | solution.py:33
  25.6 2.8 %collective-permute-done.6 = bf16[16,2048]{1,0:T(8,128)(2,1)S(1)} collective-permute-done((bf16[16,2048]{1,0:T(8,128)(2,1)S(1)}, bf16[16,2048]{1,0:T(8,128)(2,1)S(1)}, u32[]{:S(2)}, u32[]{:S(2)}) %collective-permute-start.6) | collective-permute-done | bytes 65568 | tf_op jit(solution)/shard_map/ppermute | solution.py:33
  28.4 0.1 collective-permute-start.7
  28.5 1.2 %collective-permute-done.7 = bf16[16,2048]{1,0:T(8,128)(2,1)S(1)} collective-permute-done((bf16[16,2048]{1,0:T(8,128)(2,1)S(1)}, bf16[16,2048]{1,0:T(8,128)(2,1)S(1)}, u32[]{:S(2)}, u32[]{:S(2)}) %collective-permute-start.7) | collective-permute-done | bytes 65568 | tf_op jit(solution)/shard_map/ppermute | solution.py:33
  29.7 0.6 %add_convert_fusion = bf16[16,2048]{1,0:T(8,128)(2,1)} fusion(bf16[16,2048]{1,0:T(8,128)(2,1)S(1)} %collective-permute-done.7, bf16[16,2048]{1,0:T(8,128)(2,1)S(1)} %add_convert_fusion.1), kind=kLoop, calls=%fused_computation | loop fusion | flops 131072 | bytes 196608 | tf_op jit(solution)/shard_map/convert_element_type | solution.py:342
  (1 shorter events, 0.0 us)
Async XLA Ops:
  0.6 14.8 %copy-start.2 = (bf16[4,768,2,128]{3,2,1,0:T(2,128)(2,1)S(1)}, bf16[4,768,2,128]{3,2,1,0:T(2,128)(2,1)}, u32[]{:S(2)}) copy-start(bf16[4,768,2,128]{3,2,1,0:T(2,128)(2,1)} %param.16) | copy-start | bytes 4718596
  0.6 14.8 %copy-start.1 = (bf16[4,768,2,128]{3,2,1,0:T(2,128)(2,1)S(1)}, bf16[4,768,2,128]{3,2,1,0:T(2,128)(2,1)}, u32[]{:S(2)}) copy-start(bf16[4,768,2,128]{3,2,1,0:T(2,128)(2,1)} %param.15) | copy-start | bytes 4718596
  0.7 22.0 %copy-start = (bf16[2048,2048]{1,0:T(8,128)(2,1)S(1)}, bf16[2048,2048]{1,0:T(8,128)(2,1)}, u32[]{:S(2)}) copy-start(bf16[2048,2048]{1,0:T(8,128)(2,1)} %refs_4_.3) | copy-start | bytes 25165828
  5.4 7.1 %collective-permute-start = (f32[4,2560]{1,0:T(4,128)S(1)}, f32[4,2560]{1,0:T(4,128)S(1)}, u32[]{:S(2)}, u32[]{:S(2)}) collective-permute-start(f32[4,2560]{1,0:T(4,128)S(1)} %get-tuple-element.16), channel_id=1, source_target_pairs={{0,12},{4,8},{8,4},{12,0},{1,13},{5,9},{9,5},{13,1},{2,14},{6,10},... | collective-permute-start | bytes 122888 | tf_op jit(solution)/shard_map/ppermute | solution.py:33
  10.5 4.9 %collective-permute-start.1 = (f32[4,2560]{1,0:T(4,128)S(1)}, f32[4,2560]{1,0:T(4,128)S(1)}, u32[]{:S(2)}, u32[]{:S(2)}) collective-permute-start(f32[4,2560]{1,0:T(4,128)S(1)} %get-tuple-element.17), channel_id=1, source_target_pairs={{0,8},{4,12},{8,0},{12,4},{1,9},{5,13},{9,1},{13,5},{2,10},{6,14},... | collective-permute-start | bytes 122888 | tf_op jit(solution)/shard_map/ppermute | solution.py:33
  10.5 4.9 %collective-permute-start.2 = (f32[4,2560]{1,0:T(4,128)S(1)}, f32[4,2560]{1,0:T(4,128)S(1)}, u32[]{:S(2)}, u32[]{:S(2)}) collective-permute-start(f32[4,2560]{1,0:T(4,128)S(1)} %get-tuple-element.18), channel_id=1, source_target_pairs={{0,4},{4,0},{8,12},{12,8},{1,5},{5,1},{9,13},{13,9},{2,6},{6,2},{1... | collective-permute-start | bytes 122888 | tf_op jit(solution)/shard_map/ppermute | solution.py:33
  16.3 5.6 %collective-permute-start.5 = (bf16[4,2048]{1,0:T(4,128)(2,1)S(1)}, bf16[4,2048]{1,0:T(4,128)(2,1)S(1)}, u32[]{:S(2)}, u32[]{:S(2)}) collective-permute-start(bf16[4,2048]{1,0:T(4,128)(2,1)S(1)} %get-tuple-element.23.refs_0_), channel_id=1, source_target_pairs={{0,12},{4,8},{8,4},{12,0},{1,13},{5,9},{9,5},{13,1},{2,14},{6,10},... | collective-permute-start | bytes 49160 | tf_op jit(solution)/shard_map/ppermute | solution.py:33
  18.0 4.7 %collective-permute-start.4 = (bf16[4,2048]{1,0:T(4,128)(2,1)S(1)}, bf16[4,2048]{1,0:T(4,128)(2,1)S(1)}, u32[]{:S(2)}, u32[]{:S(2)}) collective-permute-start(bf16[4,2048]{1,0:T(4,128)(2,1)S(1)} %get-tuple-element.23.refs_0_), channel_id=1, source_target_pairs={{0,8},{4,12},{8,0},{12,4},{1,9},{5,13},{9,1},{13,5},{2,10},{6,14},... | collective-permute-start | bytes 49160 | tf_op jit(solution)/shard_map/ppermute | solution.py:33
  18.5 4.2 %collective-permute-start.3 = (bf16[4,2048]{1,0:T(4,128)(2,1)S(1)}, bf16[4,2048]{1,0:T(4,128)(2,1)S(1)}, u32[]{:S(2)}, u32[]{:S(2)}) collective-permute-start(bf16[4,2048]{1,0:T(4,128)(2,1)S(1)} %get-tuple-element.23.refs_0_), channel_id=1, source_target_pairs={{0,4},{4,0},{8,12},{12,8},{1,5},{5,1},{9,13},{13,9},{2,6},{6,2},{1... | collective-permute-start | bytes 49160 | tf_op jit(solution)/shard_map/ppermute | solution.py:33
  24.1 4.3 %collective-permute-start.6 = (bf16[16,2048]{1,0:T(8,128)(2,1)S(1)}, bf16[16,2048]{1,0:T(8,128)(2,1)S(1)}, u32[]{:S(2)}, u32[]{:S(2)}) collective-permute-start(bf16[16,2048]{1,0:T(8,128)(2,1)S(1)} %get-tuple-element.24), channel_id=1, source_target_pairs={{0,2},{1,3},{2,0},{3,1},{4,6},{5,7},{6,4},{7,5},{8,10},{9,11},{10,... | collective-permute-start | bytes 196616 | tf_op jit(solution)/shard_map/ppermute | solution.py:33
  28.4 1.3 %collective-permute-start.7 = (bf16[16,2048]{1,0:T(8,128)(2,1)S(1)}, bf16[16,2048]{1,0:T(8,128)(2,1)S(1)}, u32[]{:S(2)}, u32[]{:S(2)}) collective-permute-start(bf16[16,2048]{1,0:T(8,128)(2,1)S(1)} %add_convert_fusion.1), channel_id=1, source_target_pairs={{0,1},{1,0},{2,3},{3,2},{4,5},{5,4},{6,7},{7,6},{8,9},{9,8},{10,11... | collective-permute-start | bytes 196616 | tf_op jit(solution)/shard_map/ppermute | solution.py:33
